TPU v7x, 32 devices: a whole 2x2x4 slice. The times are simulated.
32 devices in a mesh: comp: 2 (over x), tx: 4 (over z), ty: 4 (over y, core).
Axes of the slice: x: 2, y: 2, z: 4, core: 2. Of those that a mesh axis runs over, the one named last changes fastest.
Arguments:
- spectrum: float32 [1800, 32, 1024], P('comp', 'tx', 'ty'), may hold values from 0.05 to 2
- sea_mask: int32 [32, 1024], P('tx', 'ty'), may hold values from 0 to 1, as said below
- owner_list: int32 [4, 4, 8, 256], P('tx', 'ty'), may hold values from 0 to 2047, as said below
- owner_count: int32 [4, 4, 8], P('tx', 'ty'), may hold values from 0 to 256, as said below
- slopes: float32 [2, 32, 1024], P(None, 'tx', 'ty'), may hold values from -0.00015 to 0.00015
- friction: float32 [32, 1024], P('tx', 'ty'), may hold values from 0.15 to 0.6
- wind_angle: float32 [32, 1024], P('tx', 'ty'), may hold values from -3.140625 to 3.140625
Outputs:
- new_spectrum: float32 [1800, 32, 1024], P('comp', 'tx', 'ty')
Inputs may be any that keep to these rules, and one draw needn't show every extreme that they name: `sea_mask`: 1 marks sea, 0 land. Each row of tiles along tx holds a tile without land, and each latitude row of a tile has a sea cell. `owner_list`: owner o is the device of index o along comp+tx (comp slowest) in the same row of tiles. For each tile, the first owner_count slots of each owner name cells of the tile as ix * 256 + iy; together they name every sea cell of the tile exactly once and no land cell. The other slots hold 0. `owner_count`: points of one tile given to one owner, at most 256; 256 is reached in every draw.
All inputs are finite; a program needn't handle non-finite values.
Results may differ from a plain program's by a relative error of at most 0.0003.
Values sent between devices are 32-bit elements; how exact they have to be, the bound alone decides.
No kernel may reach another device: no remote copies, remote signals or barrier semaphores. Data moves between devices by JAX's collectives and lax.ppermute only.
A program may use at most 128 MiB of HBM per device.

v0:
```python
import functools
import math

import jax
import jax.numpy as jnp
from jax import lax
from jax.experimental import pallas as pl
from jax.experimental.pallas import tpu as pltpu
from jax.sharding import PartitionSpec as P

NDIR = 36
NFREQ = 50


TIME_STEP = 240.0
CELL_SIZE = 11100.0
GRAVITY = 9.81
LOW_FREQ = 0.0373
HIGH_FREQ = 1.0
WIND_GROWTH = 0.0001
WIND_FACTOR = 28.0
SATURATION_LOSS = 0.0005
CUMULATIVE_LOSS = 0.001
STEEPNESS_LOSS = 0.005
SATURATION_LEVEL = 0.6


def padded(value, sides, width, wrap):
    for axis, dim in sides:
        size, length = (lax.axis_size(axis), value.shape[dim])
        up = [(i, (i + 1) % size) for i in range(size if wrap else size - 1)]
        down = [(j, i) for i, j in up]
        last = lax.slice_in_dim(value, length - width, length, axis=dim)
        first = lax.slice_in_dim(value, 0, width, axis=dim)
        before = lax.ppermute(last, axis, up)
        after = lax.ppermute(first, axis, down)
        value = jnp.concatenate([before, value, after], axis=dim)
    return value


def freq_values(freq_ids):
    return (
        2.0
        * math.pi
        * LOW_FREQ
        * jnp.exp(freq_ids.astype(jnp.float32) * (math.log(HIGH_FREQ / LOW_FREQ) / (NFREQ - 1)))
    )


def wave_tables(first_comp, comp_count):
    comp_ids = first_comp + jnp.arange(comp_count, dtype=jnp.int32)
    headings = (comp_ids // NFREQ).astype(jnp.float32) * (2.0 * math.pi / NDIR)
    return (headings, freq_values(comp_ids % NFREQ))


def advect(
    energy,
    west_side,
    east_side,
    south_side,
    north_side,
    prev_dir,
    next_dir,
    headings,
    ang_freq,
    slopes,
):
    group_speed = GRAVITY / (2.0 * ang_freq)
    along_x = (TIME_STEP / CELL_SIZE * group_speed * jnp.cos(headings))[:, None, None]
    along_y = (TIME_STEP / CELL_SIZE * group_speed * jnp.sin(headings))[:, None, None]
    bending = TIME_STEP * NDIR / (2.0 * math.pi) * (2.0 * math.pi * LOW_FREQ) / ang_freq
    turning = bending[:, None, None] * (
        jnp.sin(headings)[:, None, None] * slopes[0][None]
        - jnp.cos(headings)[:, None, None] * slopes[1][None]
    )
    change = jnp.maximum(along_x, 0.0) * (energy - west_side) + jnp.minimum(along_x, 0.0) * (
        east_side - energy
    )
    change = (
        change
        + jnp.maximum(along_y, 0.0) * (energy - south_side)
        + jnp.minimum(along_y, 0.0) * (north_side - energy)
    )
    change = (
        change
        + jnp.maximum(turning, 0.0) * (energy - prev_dir)
        + jnp.minimum(turning, 0.0) * (next_dir - energy)
    )
    return energy - change


def source_terms(spectra, friction, wind_angle):
    dir_ids = jnp.arange(NDIR, dtype=jnp.int32)
    offset = (dir_ids[:, None] - dir_ids[None, :]) % NDIR
    nearest = jnp.minimum(offset, NDIR - offset)
    spread = jnp.where(
        4 * nearest < NDIR, jnp.cos(offset.astype(jnp.float32) * (2.0 * math.pi / NDIR)) ** 2, 0.0
    )
    spread = spread / jnp.sum(spread, axis=1, keepdims=True)
    sat_level = jnp.einsum("de,efp->dfp", spread, spectra, precision=lax.Precision.HIGHEST)
    excess = jnp.maximum(sat_level / SATURATION_LEVEL - 1.0, 0.0)
    excess_sq = excess * excess
    freq_ids = jnp.arange(NFREQ, dtype=jnp.int32)
    below_mask = (freq_ids[None, :] < freq_ids[:, None]).astype(jnp.float32)
    running = (
        jnp.einsum("fg,dgp->dfp", below_mask, excess_sq, precision=lax.Precision.HIGHEST) / NFREQ
    )
    ang_freq = freq_values(freq_ids)
    weights = (ang_freq / ang_freq[NFREQ - 1]) ** 2
    steepness = jnp.einsum("dfp,f->p", spectra, weights, precision=lax.Precision.HIGHEST) / (
        NDIR * NFREQ
    )
    headings = dir_ids.astype(jnp.float32) * (2.0 * math.pi / NDIR)
    alignment = (
        jnp.cos(headings)[:, None, None] * jnp.cos(wind_angle)[None, None, :]
        + jnp.sin(headings)[:, None, None] * jnp.sin(wind_angle)[None, None, :]
    )
    forcing = WIND_FACTOR / GRAVITY * friction[None, None, :] * ang_freq[None, :, None] * alignment
    growth = WIND_GROWTH * ang_freq[None, :, None] * jnp.maximum(forcing - 1.0, 0.0)
    losses = ang_freq[None, :, None] * (
        SATURATION_LOSS * excess_sq
        + CUMULATIVE_LOSS * running
        + STEEPNESS_LOSS * (steepness * steepness)[None, None, :]
    )
    return spectra * (1.0 + TIME_STEP * growth) / (1.0 + TIME_STEP * losses)


def shards(spectrum, sea_mask, owner_list, owner_count, slopes, friction, wind_angle):
    comp_size = lax.axis_size("comp")
    local_comps = spectrum.shape[0]
    cell_count = spectrum.shape[1] * spectrum.shape[2]
    sea_cells = sea_mask.astype(jnp.float32)
    masked = spectrum * sea_cells[None]
    headings, ang_freq = wave_tables(lax.axis_index("comp") * local_comps, local_comps)
    padded_lon = padded(masked, (("tx", 1),), 1, True)
    padded_lat = padded(masked, (("ty", 2),), 1, False)
    padded_dir = padded(masked, (("comp", 0),), NFREQ, True)
    advected = (
        advect(
            masked,
            padded_lon[:, :-2],
            padded_lon[:, 2:],
            padded_lat[:, :, :-2],
            padded_lat[:, :, 2:],
            padded_dir[:local_comps],
            padded_dir[2 * NFREQ :],
            headings,
            ang_freq,
            slopes,
        )
        * sea_cells[None]
    )
    moved_flat = advected.reshape(local_comps, cell_count)
    cell_names = owner_list[0, 0]
    slot_ids = jnp.arange(cell_names.shape[1], dtype=jnp.int32)
    in_use = slot_ids[None, :] < owner_count[0, 0][:, None]
    target = jnp.where(in_use, cell_names, cell_count).reshape(-1)
    owners = cell_names.shape[0]
    capacity = cell_names.shape[1]
    tiles_x = lax.axis_size("tx")
    cell_ids = jnp.arange(cell_count, dtype=jnp.int32)
    selector = (cell_ids[:, None] == target[None, :]).astype(jnp.float32)
    outgoing = jnp.dot(moved_flat, selector, precision=lax.Precision.HIGHEST).reshape(
        local_comps, owners, capacity
    )
    wind_rows = jnp.stack([friction.reshape(-1), wind_angle.reshape(-1)])
    point_data = jnp.dot(wind_rows, selector, precision=lax.Precision.HIGHEST).reshape(
        2, owners, capacity
    )
    spectra = lax.all_to_all(outgoing, ("comp", "tx"), split_axis=1, concat_axis=1, tiled=True)
    extras = lax.all_to_all(point_data, ("comp", "tx"), split_axis=1, concat_axis=1, tiled=True)
    batch_size = spectra.shape[2]
    full_spec = (
        spectra.reshape(local_comps, comp_size, tiles_x * batch_size)
        .transpose(1, 0, 2)
        .reshape(NDIR, NFREQ, tiles_x * batch_size)
    )
    extra_rows = extras.reshape(2, comp_size, tiles_x * batch_size)[:, 0]
    result = source_terms(full_spec, extra_rows[0], extra_rows[1])
    homeward = (
        result.reshape(comp_size, local_comps, tiles_x * batch_size)
        .transpose(1, 0, 2)
        .reshape(local_comps, comp_size * tiles_x, batch_size)
    )
    returned = lax.all_to_all(homeward, ("comp", "tx"), split_axis=1, concat_axis=1, tiled=True)
    gathered = lax.dot_general(
        returned.reshape(local_comps, owners * capacity),
        selector,
        (((1,), (1,)), ((), ())),
        precision=lax.Precision.HIGHEST,
    )
    listed = jnp.sum(selector, axis=1) > 0.5
    updated = jnp.where(listed[None], gathered, moved_flat)
    return updated.reshape(spectrum.shape)


def chunk_bounds():
    return [(5 * i, 5 * i + 5) for i in range(9)] + [(45, 47), (47, 49), (49, 50)]


HALO_GROUPS = ((0, 15), (15, 50))
SUM_CHUNKS = 3
SOURCES_DONE = {8: 2, 9: 5, 10: 7, 11: 9}
HALF_DIRS = NDIR // 2
SIDE_DIRS = 8
LEAD_DIRS = 9
VMEM_BYTES = 24 * 1024 * 1024
SMALL_COST = pl.CostEstimate(flops=1024, bytes_accessed=1024, transcendentals=0)


FREQ_STEP = (HIGH_FREQ / LOW_FREQ) ** (1.0 / (NFREQ - 1))


def frequency(index):
    return 2.0 * math.pi * LOW_FREQ * FREQ_STEP**index


def heading(index):
    return 2.0 * math.pi * index / NDIR


def raw_kernel(spec_ref, raw_ref, sems):
    copies = []
    for i, d in enumerate((0, HALF_DIRS - 1)):
        copy = pltpu.make_async_copy(spec_ref.at[d], raw_ref.at[i], sems.at[i])
        copy.start()
        copies.append(copy)
    for copy in copies:
        copy.wait()


def raw_edges(spec):
    return pl.pallas_call(
        raw_kernel,
        out_shape=jax.ShapeDtypeStruct((2, NFREQ, 8, 256), jnp.float32),
        in_specs=[pl.BlockSpec(memory_space=pl.ANY)],
        out_specs=pl.BlockSpec(memory_space=pltpu.VMEM),
        scratch_shapes=[pltpu.SemaphoreType.DMA((2,))],
        compiler_params=pltpu.CompilerParams(vmem_limit_bytes=VMEM_BYTES),
        cost_estimate=SMALL_COST,
    )(spec)


def pack_kernel(first, count, sea_ref, spec_ref, after_ref, lead_ref, trail_ref, lat_ref, held, sems):
    def body(flipped):
        lead_row, trail_row = (0, 7) if flipped else (7, 0)
        part = 0 if flipped else 1
        copies = []
        for d in range(HALF_DIRS):
            for h in range(2):
                copy = pltpu.make_async_copy(
                    spec_ref.at[d, pl.ds(first, count), :, pl.ds(128 * h, 128)], held.at[h * HALF_DIRS + d], sems.at[h * HALF_DIRS + d]
                )
                copy.start()
                copies.append(copy)
        rows = held.reshape((2 * HALF_DIRS + 1) * count * 8, 128)
        for d in range(HALF_DIRS):
            for h in range(2):
                copies[2 * d + h].wait()
                lanes_here = slice(128 * h, 128 * h + 128)
                start = (h * HALF_DIRS + d) * count * 8
                if d < LEAD_DIRS:
                    column = rows[pl.ds(start + lead_row, count, stride=8), :]
                    lead_ref[d * count : (d + 1) * count, lanes_here] = column * sea_ref[lead_row : lead_row + 1, lanes_here]
                elif d > LEAD_DIRS:
                    t = d - LEAD_DIRS - 1
                    column = rows[pl.ds(start + trail_row, count, stride=8), :]
                    trail_ref[t * count : (t + 1) * count, lanes_here] = column * sea_ref[trail_row : trail_row + 1, lanes_here]
        lane = 0 if flipped else 127
        lanes = lax.broadcasted_iota(jnp.int32, (8, 128), 1)
        sea_line = jnp.broadcast_to(sea_ref[:, 128 * part + lane : 128 * part + lane + 1], (8, 128))

        def one(f, kept):
            here = lanes == f
            return tuple(
                jnp.where(here, jnp.broadcast_to(held[part * HALF_DIRS + d, f][:, lane : lane + 1], (8, 128)), kept[d])
                for d in range(HALF_DIRS)
            )

        zeros = jnp.zeros((8, 128), jnp.float32)
        kept = lax.fori_loop(0, count, one, (zeros,) * HALF_DIRS, unroll=5)
        for d in range(HALF_DIRS):
            lat_ref[d] = kept[d] * sea_line

    half = lax.axis_index("comp")

    @pl.when(half == 0)
    def _():
        body(False)

    @pl.when(half != 0)
    def _():
        body(True)


def pack(first, count, sea, spec, after):
    vmem = pl.BlockSpec(memory_space=pltpu.VMEM)
    hold = pl.BlockSpec(memory_space=pl.ANY)
    return pl.pallas_call(
        functools.partial(pack_kernel, first, count),
        out_shape=[
            jax.ShapeDtypeStruct((LEAD_DIRS * count, 256), jnp.float32),
            jax.ShapeDtypeStruct(((HALF_DIRS - LEAD_DIRS - 1) * count, 256), jnp.float32),
            jax.ShapeDtypeStruct((HALF_DIRS, 8, 128), jnp.float32),
        ],
        in_specs=[vmem, hold, hold],
        out_specs=[vmem] * 3,
        scratch_shapes=[
            pltpu.VMEM((2 * HALF_DIRS + 1, count, 8, 128), jnp.float32),
            pltpu.SemaphoreType.DMA((2 * HALF_DIRS,)),
        ],
        compiler_params=pltpu.CompilerParams(vmem_limit_bytes=VMEM_BYTES),
        cost_estimate=SMALL_COST,
    )(sea, spec, after)


ALL_DIRS = tuple(range(HALF_DIRS))
INNER_DIRS = ALL_DIRS[1:-1]
OUTER_DIRS = (0, HALF_DIRS - 1)


def is_sent(d):
    return d < SIDE_DIRS or d >= HALF_DIRS - SIDE_DIRS


def slab_index(dirs, count, base=0):
    return {d: base + count * n for n, d in enumerate(d for d in dirs if is_sent(d))}


def advect_kernel(
    group, passes, carries, waits, has_raw,
    sea_ref, slope_ref, spec_ref, lead_ref, trail_ref, lat_ref, steep_ref, *rest,
):
    sums = any(summed for *_, summed in passes)
    raw_ref = rest[0] if has_raw else None
    rest = rest[has_raw + waits :]
    held, turn, sem = rest[-3:]
    send_ref, keep_ref = rest[:2]
    if sums:
        steep_out_ref = rest[-4]
    copies, base = [], 0
    for i, (first, count, *_) in enumerate(passes):
        copy = pltpu.make_async_copy(spec_ref.at[:, pl.ds(first, count)], held.at[:, pl.ds(base, count)], sem.at[i])
        copy.start()
        copies.append(copy)
        base += count
    for d in range(HALF_DIRS):
        turn[d] = math.sin(heading(d)) * slope_ref[0] - math.cos(heading(d)) * slope_ref[1]
    if sums:
        steep_out_ref[...] = steep_ref[...]
    for copy in copies:
        copy.wait()
    rows_at = lax.broadcasted_iota(jnp.int32, (8, 256), 0)
    lanes_at = lax.broadcasted_iota(jnp.int32, (8, 256), 1)
    per_cell = TIME_STEP / CELL_SIZE * GRAVITY / 2.0
    bending = TIME_STEP * NDIR / (2.0 * math.pi) * (2.0 * math.pi * LOW_FREQ)
    group_count = group[1] - group[0]

    def body(flipped):
        lead_row, lead_shift = (7, 7) if flipped else (0, 1)
        trail_row, trail_shift = (0, 1) if flipped else (7, 7)
        lat_lane, lat_shift = (255, 255) if flipped else (0, 1)

        def one(first, dirs, slabs, summed, base, f, factors):
            sea = sea_ref[...]
            inverse, weight = factors
            total = jnp.zeros((8, 256), jnp.float32)
            offset = first - group[0]

            def energy(d):
                if d < 0:
                    return raw_ref[1, first + f] * sea
                if d >= HALF_DIRS:
                    return raw_ref[0, first + f] * sea
                return held[d, base + f] * sea

            known = {}
            for d in dirs:
                known = {e: known[e] if e in known else energy(e) for e in (d - 1, d, d + 1)}
                prev, here, after = known[d - 1], known[d], known[d + 1]
                rate = turn[d]
                size = jnp.abs(rate) * bending
                moved = size * jnp.where(rate > 0.0, prev, after)
                along_x = per_cell * abs(math.cos(heading(d)))
                along_y = per_cell * abs(math.sin(heading(d)))
                fixed = 0.0
                if d != LEAD_DIRS:
                    if d < LEAD_DIRS:
                        row = lead_ref[pl.ds(d * group_count + offset + f, 1), :]
                        edge, shift = lead_row, lead_shift
                    else:
                        row = trail_ref[pl.ds((d - LEAD_DIRS - 1) * group_count + offset + f, 1), :]
                        edge, shift = trail_row, trail_shift
                    side = jnp.where(rows_at == edge, jnp.broadcast_to(row, (8, 256)), pltpu.roll(here, shift, 0))
                    moved = moved + along_x * side
                    fixed += along_x
                if d != 0:
                    halo = pltpu.roll(lat_ref[d], lax.rem((lat_lane % 128) + 128 - (offset + f), 128), 1)
                    halo = jnp.concatenate([halo, halo], axis=1)
                    side = jnp.where(lanes_at == lat_lane, halo, pltpu.roll(here, lat_shift, 1))
                    moved = moved + along_y * side
                    fixed += along_y
                result = (here - inverse * ((size + fixed) * here - moved)) * sea
                if slabs is not None and is_sent(d):
                    send_ref[slabs[d] + f] = result
                elif slabs is not None:
                    keep_ref[d - SIDE_DIRS, f] = result
                total = total + result
            if summed:
                steep_out_ref[...] += weight * total
            return inverse * (1.0 / FREQ_STEP), weight * FREQ_STEP**2

        base = 0
        for first, count, dirs, slabs, summed in passes:
            factors = jnp.float32(1.0 / frequency(first)), jnp.float32((frequency(first) / frequency(NFREQ - 1)) ** 2)
            lax.fori_loop(0, count, functools.partial(one, first, dirs, slabs, summed, base), factors)
            base += count

    half = lax.axis_index("comp")

    @pl.when(half == 0)
    def _():
        body(False)

    @pl.when(half != 0)
    def _():
        body(True)

    if carries:
        send_ref[send_ref.shape[0] - 1] = steep_out_ref[...]


def advect_chunk(passes, group, carries, sea, slopes, spec, sides, steep, raw, after):
    vmem = pl.BlockSpec(memory_space=pltpu.VMEM)
    hold = pl.BlockSpec(memory_space=pl.ANY)
    slabs = sum(count * len(place) for _, count, _, place, _ in passes if place is not None)
    raw = () if raw is None else (raw,)
    out_shape = [
        jax.ShapeDtypeStruct((slabs + carries, 8, 256), jnp.float32),
        jax.ShapeDtypeStruct((HALF_DIRS - 2 * SIDE_DIRS, passes[0][1], 8, 256), jnp.float32),
    ]
    if any(summed for *_, summed in passes):
        out_shape.append(jax.ShapeDtypeStruct((8, 256), jnp.float32))
    return pl.pallas_call(
        functools.partial(advect_kernel, group, passes, carries, len(after), len(raw)),
        out_shape=out_shape,
        in_specs=[vmem, vmem, hold, vmem, vmem, vmem, vmem] + [vmem] * len(raw) + [hold] * len(after),
        out_specs=[vmem] * len(out_shape),
        scratch_shapes=[
            pltpu.VMEM((HALF_DIRS, sum(p[1] for p in passes), 8, 256), jnp.float32),
            pltpu.VMEM((HALF_DIRS, 8, 256), jnp.float32),
            pltpu.SemaphoreType.DMA((len(passes),)),
        ],
        compiler_params=pltpu.CompilerParams(vmem_limit_bytes=VMEM_BYTES),
        cost_estimate=SMALL_COST,
    )(sea, slopes, spec, *sides, steep, *raw, *after)


def source_kernel(
    first, count, inner, outer, chained, last,
    wind_ref, steep_a_ref, steep_b_ref, cum_ref, own_ref, keep_ref, other_ref, *rest,
):
    edge_own_ref, edge_other_ref = rest[:2] if outer else (None, None)
    out_ref, cum_out_ref, result, align, sems = rest[(2 if outer else 0) + chained :]
    weights = [math.cos(heading(m)) ** 2 / (9.0 * SATURATION_LEVEL) for m in range(SIDE_DIRS + 1)]
    steep = (steep_a_ref[...] + steep_b_ref[...]) * (1.0 / (NDIR * NFREQ))
    steep_sq = steep * steep
    for d in range(HALF_DIRS):
        align[d] = math.cos(heading(d)) * wind_ref[0] + math.sin(heading(d)) * wind_ref[1]
    cum_out_ref[...] = cum_ref[...]

    def leave(f):
        return pltpu.make_async_copy(result.at[:, f], out_ref.at[:, first + f], sems.at[f])

    def one(f, omega):
        gain = TIME_STEP * WIND_GROWTH * omega
        loss_sat = TIME_STEP * SATURATION_LOSS * omega
        loss_cum = TIME_STEP * CUMULATIVE_LOSS / NFREQ * omega
        loss_steep = TIME_STEP * STEEPNESS_LOSS * omega
        for half in range(2):
            lanes = slice(128 * half, 128 * half + 128)

            def slab(d, main, edge):
                return main[inner[d] + f, :, lanes] if d in inner else edge[outer[d] + f, :, lanes]

            first_dirs, last_dirs = ALL_DIRS[:SIDE_DIRS], ALL_DIRS[-SIDE_DIRS:]
            line = [slab(d, other_ref, edge_other_ref) for d in last_dirs]
            line += [slab(d, own_ref, edge_own_ref) for d in first_dirs]
            line += [keep_ref[i, f, :, lanes] for i in range(HALF_DIRS - 2 * SIDE_DIRS)]
            line += [slab(d, own_ref, edge_own_ref) for d in last_dirs]
            line += [slab(d, other_ref, edge_other_ref) for d in first_dirs]
            base = 1.0 + loss_steep * steep_sq[:, lanes]
            for d in range(HALF_DIRS):
                at = d + SIDE_DIRS
                level = weights[0] * line[at] - 1.0
                for m in range(1, SIDE_DIRS + 1):
                    level = level + weights[m] * (line[at - m] + line[at + m])
                excess = jnp.maximum(level, 0.0)
                square = excess * excess
                cum = cum_out_ref[d, :, lanes]
                cum_out_ref[d, :, lanes] = cum + square
                grown = 1.0 + gain * jnp.maximum(align[d, :, lanes] * omega - 1.0, 0.0)
                lost = base + loss_sat * square + loss_cum * cum
                result[d, f, :, lanes] = line[at] * grown / lost
        leave(f).start()
        return omega * FREQ_STEP

    lax.fori_loop(0, count, one, jnp.float32(frequency(first)))
    for f in range(count):
        leave(f).wait()


def source_chunk(first, count, inner, outer, last, wind, steep_own, steep_other, cum, own, keep, other, edges, out):
    vmem = pl.BlockSpec(memory_space=pltpu.VMEM)
    hold = pl.BlockSpec(memory_space=pl.ANY)
    chained = out is not None
    operands = (wind, steep_own, steep_other, cum, own, keep, other, *edges) + ((out,) if chained else ())
    out_shape = [jax.ShapeDtypeStruct((HALF_DIRS, NFREQ, 8, 256), jnp.float32)]
    running = [] if last else [jax.ShapeDtypeStruct((HALF_DIRS, 8, 256), jnp.float32)]
    result = pl.pallas_call(
        functools.partial(source_kernel, first, count, inner, outer, chained, last),
        out_shape=out_shape + running,
        in_specs=[vmem] * (7 + len(edges)) + [hold] * chained,
        out_specs=[hold] + [vmem] * len(running),
        scratch_shapes=[pltpu.VMEM((HALF_DIRS, 8, 256), jnp.float32)] * last
        + [
            pltpu.VMEM((HALF_DIRS, count, 8, 256), jnp.float32),
            pltpu.VMEM((HALF_DIRS, 8, 256), jnp.float32),
            pltpu.SemaphoreType.DMA((count,)),
        ],
        input_output_aliases={len(operands) - 1: 0} if chained else {},
        compiler_params=pltpu.CompilerParams(vmem_limit_bytes=VMEM_BYTES),
        cost_estimate=SMALL_COST,
    )(*operands)
    return result[0], None if last else result[1]


def ring_pairs(size, step, wrap):
    return [(i, (i + step) % size) for i in range(size) if wrap or 0 <= i + step < size]


def paired_shards(spectrum, sea_mask, owner_list, owner_count, slopes, friction, wind_angle):
    tiles_x, tiles_y = lax.axis_size("tx"), lax.axis_size("ty")
    half = lax.axis_index("comp")
    sign = 1.0 - 2.0 * half.astype(jnp.float32)
    spec = spectrum.reshape(HALF_DIRS, NFREQ, 8, 256)
    sea = sea_mask.astype(jnp.float32)
    turn = slopes * sign
    wind = (sign * WIND_FACTOR / GRAVITY) * friction * jnp.stack([jnp.cos(wind_angle), jnp.sin(wind_angle)])

    def joined(axis_size, step, wrap):
        ahead = ring_pairs(axis_size, step, wrap)
        back = ring_pairs(axis_size, -step, wrap)
        return ahead + [(axis_size + i, axis_size + j) for i, j in back]

    swap = [(0, 1), (1, 0)]
    lead_pairs = joined(tiles_x, 1, True)
    trail_pairs = joined(tiles_x, -1, True)
    lat_pairs = joined(tiles_y, 1, False)

    spec = pltpu.with_memory_space_constraint(spec, pltpu.HBM)
    bounds = chunk_bounds()
    raw = raw_edges(spec)

    def halo(g, after):
        begin, end = HALO_GROUPS[g]
        lead, trail, lat = pack(begin, end - begin, sea, spec, after)
        sides = (
            lax.ppermute(lead, ("comp", "tx"), lead_pairs),
            lax.ppermute(trail, ("comp", "tx"), trail_pairs),
            lax.ppermute(lat, ("comp", "ty"), lat_pairs),
        )
        return sides, lead

    first_sides, _ = halo(0, raw)
    raw = lax.ppermute(raw, "comp", swap)
    early = sum(end <= HALO_GROUPS[0][1] for _, end in bounds)
    counts = [end - begin for begin, end in bounds]
    places = [slab_index(INNER_DIRS if i == 0 else ALL_DIRS, counts[i]) for i in range(len(bounds))]
    edge_place = slab_index(OUTER_DIRS, counts[0], base=2 * SIDE_DIRS * counts[1])

    def advect(passes, sides, carries, steep, raw, after):
        group = HALO_GROUPS[0] if sides is first_sides else HALO_GROUPS[1]
        return advect_chunk(passes, group, carries, sea, turn, spec, sides, steep, raw, after)

    sent, kept, received, sums = [], [], [], []

    def send(result):
        sent.append(result[0])
        kept.append(result[1])
        received.append(lax.ppermute(result[0], "comp", swap))

    def source(upto):
        for j in range(len(sums), upto):
            outer, edges = (edge_place, (sent[1], received[1])) if j == 0 else (None, ())
            state[:] = source_chunk(
                bounds[j][0], counts[j], places[j], outer, j == len(bounds) - 1, wind, steep, steep_other,
                state[1], sent[j], kept[j], received[j], edges, state[0],
            )
            sums.append(state[1])

    steep = jnp.zeros((8, 256), jnp.float32)
    for i in range(early):
        passes = [(bounds[i][0], counts[i], INNER_DIRS if i == 0 else ALL_DIRS, places[i], True)]
        after = ()
        if i == 1:
            passes.append((bounds[0][0], counts[0], OUTER_DIRS, edge_place, True))
        if i >= 2:
            after = (received[i - 2], packed)
        result = advect(passes, first_sides, False, steep, raw if i else None, after)
        send(result)
        steep = result[2]
        if i == 1:
            later_sides, packed = halo(1, steep)
    state = [None, jnp.zeros((HALF_DIRS, 8, 256), jnp.float32)]
    summing = SUM_CHUNKS
    ahead = bounds[early + summing][0]
    cuts = [ahead + (NFREQ - ahead) * n // summing for n in range(summing + 1)]
    for i in range(early, len(bounds)):
        after = (received[i - 2],)
        if i in SOURCES_DONE:
            source(SOURCES_DONE[i])
            after += (sums[-1],)
        n = i - early
        passes = [(bounds[i][0], counts[i], ALL_DIRS, places[i], n < summing)]
        if n < summing:
            passes.append((cuts[n], cuts[n + 1] - cuts[n], ALL_DIRS, None, True))
        result = advect(passes, later_sides, n == summing - 1, steep, raw, after)
        send(result)
        if n < summing:
            steep = result[2]
        if n == summing - 1:
            steep_other = received[i][-1]
    source(len(bounds))
    out = state[0]
    return out.reshape(spectrum.shape)


def fits_pairs(mesh, spectrum):
    return (
        mesh.shape["comp"] == 2
        and spectrum.shape[0] == NDIR * NFREQ
        and spectrum.shape[1] == 8 * mesh.shape["tx"]
        and spectrum.shape[2] == 256 * mesh.shape["ty"]
    )


def solution(mesh):
    in_specs = (
        P("comp", "tx", "ty"),
        P("tx", "ty"),
        P("tx", "ty", None, None),
        P("tx", "ty", None),
        P(None, "tx", "ty"),
        P("tx", "ty"),
        P("tx", "ty"),
    )
    out_specs = P("comp", "tx", "ty")

    def step(spectrum, *others):
        body = paired_shards if fits_pairs(mesh, spectrum) else shards
        mapped = jax.shard_map(body, mesh=mesh, in_specs=in_specs, out_specs=out_specs, check_vma=False)
        return mapped(spectrum, *others)

    return step
```

profile of v0, /device:TPU:0, one launch (start us, length us, event | category | flops | bytes accessed | tf_op | source)
XLA Modules:
  0.0 163.9 jit_solution(17445431714490530505)
XLA Ops:
  1.2 3.0 %collective-permute-start.3 = (f32[2,50,8,256]{3,2,1,0:T(8,128)S(1)}, f32[2,50,8,256]{3,2,1,0:T(8,128)S(1)}, u32[]{:S(2)}, u32[]{:S(2)}) collective-permute-start(f32[2,50,8,256]{3,2,1,0:T(8,128)S(1)} %shard_map.55.after_ref), channel_id=1, source_target_pairs={{0,16},{16,0},{1,17},{17,1},{2,18},{18,2},{3,19},{19,3},{4,20},{20... | collective-permute-start | bytes 2457608 | tf_op jit(solution)/shard_map/ppermute | solution.py:576
  4.2 2.5 %shard_map.56 = (f32[135,256]{1,0:T(8,128)S(1)}, f32[120,256]{1,0:T(8,128)S(1)}, f32[18,8,128]{2,1,0:T(8,128)S(1)}) custom-call(f32[8,256]{1,0:T(8,128)S(1)} %convert_element_type.7.sea_ref, f32[18,50,8,256]{3,2,1,0:T(8,128)} %bitcast.9, f32[2,50,8,256]{3,2,1,0:T(8,128)S(1)} %shard_map.55.after_ref), custom_call_target="tpu_custom_call" | custom-call | flops 1024 | bytes 1024 | tf_op jit(solution)/shard_map/pallas_call | solution.py:299
  8.3 2.2 %collective-permute-start.1 = (f32[120,256]{1,0:T(8,128)S(1)}, f32[120,256]{1,0:T(8,128)S(1)}, u32[]{:S(2)}, u32[]{:S(2)}) collective-permute-start(f32[120,256]{1,0:T(8,128)S(1)} %get-tuple-element.64), channel_id=1, source_target_pairs={{0,12},{4,0},{8,4},{12,8},{16,20},{20,24},{24,28},{28,16},{1,13},{... | collective-permute-start | bytes 368648 | tf_op jit(solution)/shard_map/ppermute | solution.py:570
  12.7 3.1 %collective-permute-done.1.trail_ref = f32[120,256]{1,0:T(8,128)S(1)} collective-permute-done((f32[120,256]{1,0:T(8,128)S(1)}, f32[120,256]{1,0:T(8,128)S(1)}, u32[]{:S(2)}, u32[]{:S(2)}) %collective-permute-start.1) | collective-permute-done | bytes 122912 | tf_op jit(solution)/shard_map/ppermute | solution.py:570
  19.4 3.8 %collective-permute-done.3.rest_0_ = f32[2,50,8,256]{3,2,1,0:T(8,128)S(1)} collective-permute-done((f32[2,50,8,256]{3,2,1,0:T(8,128)S(1)}, f32[2,50,8,256]{3,2,1,0:T(8,128)S(1)}, u32[]{:S(2)}, u32[]{:S(2)}) %collective-permute-start.3) | collective-permute-done | bytes 819232 | tf_op jit(solution)/shard_map/ppermute | solution.py:576
  23.2 2.5 %shard_map.58 = (f32[90,8,256]{2,1,0:T(8,128)S(1)}, f32[2,5,8,256]{3,2,1,0:T(8,128)S(1)}, f32[8,256]{1,0:T(8,128)S(1)}) custom-call(f32[8,256]{1,0:T(8,128)S(1)} %convert_element_type.7.sea_ref, f32[2,8,256]{2,1,0:T(8,128)S(1)} %broadcast_multiply_fusion.slope_ref, f32[18,50,8,256]{3,2,1,0:T(8,128)} %bitcast.11, ...), custom_call_target="tpu_custom_call" | custom-call | flops 1024 | bytes 1024 | tf_op jit(solution)/shard_map/pallas_call | solution.py:444
  25.7 2.1 %collective-permute-start.8 = (f32[90,8,256]{2,1,0:T(8,128)S(1)}, f32[90,8,256]{2,1,0:T(8,128)S(1)}, u32[]{:S(2)}, u32[]{:S(2)}) collective-permute-start(f32[90,8,256]{2,1,0:T(8,128)S(1)} %get-tuple-element.73.rest_0_.own_ref), channel_id=1, source_target_pairs={{0,16},{16,0},{1,17},{17,1},{2,18},{18,2},{3,19},{19,3},{4,20},{20... | collective-permute-start | bytes 2211848 | tf_op jit(solution)/shard_map/ppermute | solution.py:591
  27.8 4.1 %shard_map.59 = (f32[315,256]{1,0:T(8,128)S(1)}, f32[280,256]{1,0:T(8,128)S(1)}, f32[18,8,128]{2,1,0:T(8,128)S(1)}) custom-call(f32[8,256]{1,0:T(8,128)S(1)} %convert_element_type.7.sea_ref, f32[18,50,8,256]{3,2,1,0:T(8,128)} %bitcast.12, f32[8,256]{1,0:T(8,128)S(1)} %get-tuple-element.67.after_ref.steep_ref), custom_call_target="tpu_custom_call" | custom-call | flops 1024 | bytes 1024 | tf_op jit(solution)/shard_map/pallas_call | solution.py:299
  31.9 3.6 %collective-permute-done.7.rest_1_.other_ref = f32[70,8,256]{2,1,0:T(8,128)S(1)} collective-permute-done((f32[70,8,256]{2,1,0:T(8,128)S(1)}, f32[70,8,256]{2,1,0:T(8,128)S(1)}, u32[]{:S(2)}, u32[]{:S(2)}) %collective-permute-start.7) | collective-permute-done | bytes 573472 | tf_op jit(solution)/shard_map/ppermute | solution.py:591
  35.5 2.0 %shard_map.60 = (f32[80,8,256]{2,1,0:T(8,128)S(1)}, f32[2,5,8,256]{3,2,1,0:T(8,128)S(1)}, f32[8,256]{1,0:T(8,128)S(1)}) custom-call(f32[8,256]{1,0:T(8,128)S(1)} %convert_element_type.7.sea_ref, f32[2,8,256]{2,1,0:T(8,128)S(1)} %broadcast_multiply_fusion.slope_ref, f32[18,50,8,256]{3,2,1,0:T(8,128)} %bitcast.13, ...), custom_call_target="tpu_custom_call" | custom-call | flops 1024 | bytes 1024 | tf_op jit(solution)/shard_map/pallas_call | solution.py:444
  37.6 2.1 %collective-permute-start.9 = (f32[80,8,256]{2,1,0:T(8,128)S(1)}, f32[80,8,256]{2,1,0:T(8,128)S(1)}, u32[]{:S(2)}, u32[]{:S(2)}) collective-permute-start(f32[80,8,256]{2,1,0:T(8,128)S(1)} %get-tuple-element.75.own_ref), channel_id=1, source_target_pairs={{0,16},{16,0},{1,17},{17,1},{2,18},{18,2},{3,19},{19,3},{4,20},{20... | collective-permute-start | bytes 1966088 | tf_op jit(solution)/shard_map/ppermute | solution.py:591
  41.3 2.2 %collective-permute-start.5 = (f32[280,256]{1,0:T(8,128)S(1)}, f32[280,256]{1,0:T(8,128)S(1)}, u32[]{:S(2)}, u32[]{:S(2)}) collective-permute-start(f32[280,256]{1,0:T(8,128)S(1)} %get-tuple-element.69), channel_id=1, source_target_pairs={{0,12},{4,0},{8,4},{12,8},{16,20},{20,24},{24,28},{28,16},{1,13},{... | collective-permute-start | bytes 860168 | tf_op jit(solution)/shard_map/ppermute | solution.py:570
  45.7 8.6 %collective-permute-done.5.trail_ref = f32[280,256]{1,0:T(8,128)S(1)} collective-permute-done((f32[280,256]{1,0:T(8,128)S(1)}, f32[280,256]{1,0:T(8,128)S(1)}, u32[]{:S(2)}, u32[]{:S(2)}) %collective-permute-start.5) | collective-permute-done | bytes 286752 | tf_op jit(solution)/shard_map/ppermute | solution.py:570
  54.3 3.8 %shard_map.61 = (f32[80,8,256]{2,1,0:T(8,128)}, f32[2,5,8,256]{3,2,1,0:T(8,128)S(1)}, f32[8,256]{1,0:T(8,128)S(1)}) custom-call(f32[8,256]{1,0:T(8,128)S(1)} %convert_element_type.7.sea_ref, f32[2,8,256]{2,1,0:T(8,128)S(1)} %broadcast_multiply_fusion.slope_ref, f32[18,50,8,256]{3,2,1,0:T(8,128)} %bitcast.14, f32[315,256]{1,0:T(8,128)S(1)} %collective-permute-done.4.lead_ref, ...), custom_call_target="tpu_custom_call" | custom-call | flops 1024 | bytes 1024 | tf_op jit(solution)/shard_map/pallas_call | solution.py:444
  59.4 6.0 %collective-permute-done.9.rest_1_.other_ref = f32[80,8,256]{2,1,0:T(8,128)S(1)} collective-permute-done((f32[80,8,256]{2,1,0:T(8,128)S(1)}, f32[80,8,256]{2,1,0:T(8,128)S(1)}, u32[]{:S(2)}, u32[]{:S(2)}) %collective-permute-start.9) | collective-permute-done | bytes 655392 | tf_op jit(solution)/shard_map/ppermute | solution.py:591
  65.4 4.0 %shard_map.62 = (f32[80,8,256]{2,1,0:T(8,128)}, f32[2,5,8,256]{3,2,1,0:T(8,128)S(1)}, f32[8,256]{1,0:T(8,128)S(1)}) custom-call(f32[8,256]{1,0:T(8,128)S(1)} %convert_element_type.7.sea_ref, f32[2,8,256]{2,1,0:T(8,128)S(1)} %broadcast_multiply_fusion.slope_ref, f32[18,50,8,256]{3,2,1,0:T(8,128)} %bitcast.15, f32[315,256]{1,0:T(8,128)S(1)} %collective-permute-done.4.lead_ref, ...), custom_call_target="tpu_custom_call" | custom-call | flops 1024 | bytes 1024 | tf_op jit(solution)/shard_map/pallas_call | solution.py:444
  70.2 2.1 %collective-permute-start.12 = (f32[80,8,256]{2,1,0:T(8,128)}, f32[80,8,256]{2,1,0:T(8,128)}, u32[]{:S(2)}, u32[]{:S(2)}) collective-permute-start(f32[80,8,256]{2,1,0:T(8,128)} %get-tuple-element.91.own_ref), channel_id=1, source_target_pairs={{0,16},{16,0},{1,17},{17,1},{2,18},{18,2},{3,19},{19,3},{4,20},{20... | collective-permute-start | bytes 1966088 | tf_op jit(solution)/shard_map/ppermute | solution.py:591
  72.3 7.2 %collective-permute-done.10.rest_1_.other_ref = f32[80,8,256]{2,1,0:T(8,128)} collective-permute-done((f32[80,8,256]{2,1,0:T(8,128)}, f32[80,8,256]{2,1,0:T(8,128)}, u32[]{:S(2)}, u32[]{:S(2)}) %collective-permute-start.10) | collective-permute-done | bytes 655392 | tf_op jit(solution)/shard_map/ppermute | solution.py:591
  79.5 3.1 %shard_map.63 = (f32[81,8,256]{2,1,0:T(8,128)S(1)}, f32[2,5,8,256]{3,2,1,0:T(8,128)S(1)}, f32[8,256]{1,0:T(8,128)S(1)}) custom-call(f32[8,256]{1,0:T(8,128)S(1)} %convert_element_type.7.sea_ref, f32[2,8,256]{2,1,0:T(8,128)S(1)} %broadcast_multiply_fusion.slope_ref, f32[18,50,8,256]{3,2,1,0:T(8,128)} %bitcast.16, ...), custom_call_target="tpu_custom_call" | custom-call | flops 1024 | bytes 1024 | tf_op jit(solution)/shard_map/pallas_call | solution.py:444
  82.7 2.1 %collective-permute-start.11 = (f32[81,8,256]{2,1,0:T(8,128)S(1)}, f32[81,8,256]{2,1,0:T(8,128)S(1)}, u32[]{:S(2)}, u32[]{:S(2)}) collective-permute-start(f32[81,8,256]{2,1,0:T(8,128)S(1)} %get-tuple-element.79.own_ref), channel_id=1, source_target_pairs={{0,16},{16,0},{1,17},{17,1},{2,18},{18,2},{3,19},{19,3},{4,20},{20... | collective-permute-start | bytes 1990664 | tf_op jit(solution)/shard_map/ppermute | solution.py:591
  84.9 8.7 %collective-permute-done.12.other_ref.rest_1_ = f32[80,8,256]{2,1,0:T(8,128)} collective-permute-done((f32[80,8,256]{2,1,0:T(8,128)}, f32[80,8,256]{2,1,0:T(8,128)}, u32[]{:S(2)}, u32[]{:S(2)}) %collective-permute-start.12) | collective-permute-done | bytes 655392 | tf_op jit(solution)/shard_map/ppermute | solution.py:591
  95.5 2.1 %collective-permute-start.13 = (f32[80,8,256]{2,1,0:T(8,128)S(1)}, f32[80,8,256]{2,1,0:T(8,128)S(1)}, u32[]{:S(2)}, u32[]{:S(2)}) collective-permute-start(f32[80,8,256]{2,1,0:T(8,128)S(1)} %get-tuple-element.98.own_ref), channel_id=1, source_target_pairs={{0,16},{16,0},{1,17},{17,1},{2,18},{18,2},{3,19},{19,3},{4,20},{20... | collective-permute-start | bytes 1966088 | tf_op jit(solution)/shard_map/ppermute | solution.py:591
  97.6 10.1 %collective-permute-done.11.other_ref.rest_1_ = f32[81,8,256]{2,1,0:T(8,128)S(1)} collective-permute-done((f32[81,8,256]{2,1,0:T(8,128)S(1)}, f32[81,8,256]{2,1,0:T(8,128)S(1)}, u32[]{:S(2)}, u32[]{:S(2)}) %collective-permute-start.11) | collective-permute-done | bytes 663584 | tf_op jit(solution)/shard_map/ppermute | solution.py:591
  109.5 2.1 %collective-permute-start.14 = (f32[80,8,256]{2,1,0:T(8,128)S(1)}, f32[80,8,256]{2,1,0:T(8,128)S(1)}, u32[]{:S(2)}, u32[]{:S(2)}) collective-permute-start(f32[80,8,256]{2,1,0:T(8,128)S(1)} %get-tuple-element.102.own_ref), channel_id=1, source_target_pairs={{0,16},{16,0},{1,17},{17,1},{2,18},{18,2},{3,19},{19,3},{4,20},{20... | collective-permute-start | bytes 1966088 | tf_op jit(solution)/shard_map/ppermute | solution.py:591
  115.3 6.4 %collective-permute-done.13.other_ref.rest_1_ = f32[80,8,256]{2,1,0:T(8,128)S(1)} collective-permute-done((f32[80,8,256]{2,1,0:T(8,128)S(1)}, f32[80,8,256]{2,1,0:T(8,128)S(1)}, u32[]{:S(2)}, u32[]{:S(2)}) %collective-permute-start.13) | collective-permute-done | bytes 655392 | tf_op jit(solution)/shard_map/ppermute | solution.py:591
  123.6 2.1 %collective-permute-start.15 = (f32[80,8,256]{2,1,0:T(8,128)S(1)}, f32[80,8,256]{2,1,0:T(8,128)S(1)}, u32[]{:S(2)}, u32[]{:S(2)}) collective-permute-start(f32[80,8,256]{2,1,0:T(8,128)S(1)} %get-tuple-element.106.own_ref), channel_id=1, source_target_pairs={{0,16},{16,0},{1,17},{17,1},{2,18},{18,2},{3,19},{19,3},{4,20},{20... | collective-permute-start | bytes 1966088 | tf_op jit(solution)/shard_map/ppermute | solution.py:591
  127.5 3.1 %shard_map.67 = (f32[18,50,8,256]{3,2,1,0:T(8,128)}, f32[18,8,256]{2,1,0:T(8,128)S(1)}) custom-call(f32[2,8,256]{2,1,0:T(8,128)S(1)} %maximum_multiply_fusion.wind_ref, f32[8,256]{1,0:T(8,128)S(1)} %get-tuple-element.78.steep_a_ref.steep_ref, f32[8,256]{1,0:T(8,128)S(1)} %slice_bitcast_fusion.steep_b_ref, ...), custom_call_target="tpu_custom_call", output_to_operand_aliasing={{0}: (7, {})} | custom-call | flops 1024 | bytes 1024 | tf_op jit(solution)/shard_map/pallas_call | solution.py:520
  130.6 3.1 %shard_map.68 = (f32[18,50,8,256]{3,2,1,0:T(8,128)}, f32[18,8,256]{2,1,0:T(8,128)S(1)}) custom-call(f32[2,8,256]{2,1,0:T(8,128)S(1)} %maximum_multiply_fusion.wind_ref, f32[8,256]{1,0:T(8,128)S(1)} %get-tuple-element.78.steep_a_ref.steep_ref, f32[8,256]{1,0:T(8,128)S(1)} %slice_bitcast_fusion.steep_b_ref, ...), custom_call_target="tpu_custom_call", output_to_operand_aliasing={{0}: (7, {})} | custom-call | flops 1024 | bytes 1024 | tf_op jit(solution)/shard_map/pallas_call | solution.py:520
  133.7 2.1 %collective-permute-done.14.other_ref.rest_1_ = f32[80,8,256]{2,1,0:T(8,128)S(1)} collective-permute-done((f32[80,8,256]{2,1,0:T(8,128)S(1)}, f32[80,8,256]{2,1,0:T(8,128)S(1)}, u32[]{:S(2)}, u32[]{:S(2)}) %collective-permute-start.14) | collective-permute-done | bytes 655392 | tf_op jit(solution)/shard_map/ppermute | solution.py:591
  137.0 2.1 %collective-permute-start.16 = (f32[32,8,256]{2,1,0:T(8,128)S(1)}, f32[32,8,256]{2,1,0:T(8,128)S(1)}, u32[]{:S(2)}, u32[]{:S(2)}) collective-permute-start(f32[32,8,256]{2,1,0:T(8,128)S(1)} %get-tuple-element.110.own_ref), channel_id=1, source_target_pairs={{0,16},{16,0},{1,17},{17,1},{2,18},{18,2},{3,19},{19,3},{4,20},{20... | collective-permute-start | bytes 786440 | tf_op jit(solution)/shard_map/ppermute | solution.py:591
  142.8 7.0 %collective-permute-done.15.other_ref.rest_1_ = f32[80,8,256]{2,1,0:T(8,128)S(1)} collective-permute-done((f32[80,8,256]{2,1,0:T(8,128)S(1)}, f32[80,8,256]{2,1,0:T(8,128)S(1)}, u32[]{:S(2)}, u32[]{:S(2)}) %collective-permute-start.15) | collective-permute-done | bytes 655392 | tf_op jit(solution)/shard_map/ppermute | solution.py:591
  151.1 2.1 %collective-permute-start.17 = (f32[32,8,256]{2,1,0:T(8,128)S(1)}, f32[32,8,256]{2,1,0:T(8,128)S(1)}, u32[]{:S(2)}, u32[]{:S(2)}) collective-permute-start(f32[32,8,256]{2,1,0:T(8,128)S(1)} %get-tuple-element.114.own_ref), channel_id=1, source_target_pairs={{0,16},{16,0},{1,17},{17,1},{2,18},{18,2},{3,19},{19,3},{4,20},{20... | collective-permute-start | bytes 786440 | tf_op jit(solution)/shard_map/ppermute | solution.py:591
  (69 shorter events, 42.3 us)
Async XLA Ops:
  0.0 4.2 %copy-start.12 = (s32[8,256]{1,0:T(8,128)S(1)}, s32[8,256]{1,0:T(8,128)}, u32[]{:S(2)}) copy-start(s32[8,256]{1,0:T(8,128)} %param.8) | copy-start | bytes 24580
  0.0 11.8 %copy-start.10 = (f32[2,8,256]{2,1,0:T(8,128)S(1)}, f32[2,8,256]{2,1,0:T(8,128)}, u32[]{:S(2)}) copy-start(f32[2,8,256]{2,1,0:T(8,128)} %param.9) | copy-start | bytes 49156
  1.2 22.1 %collective-permute-start.3 = (f32[2,50,8,256]{3,2,1,0:T(8,128)S(1)}, f32[2,50,8,256]{3,2,1,0:T(8,128)S(1)}, u32[]{:S(2)}, u32[]{:S(2)}) collective-permute-start(f32[2,50,8,256]{3,2,1,0:T(8,128)S(1)} %shard_map.55.after_ref), channel_id=1, source_target_pairs={{0,16},{16,0},{1,17},{17,1},{2,18},{18,2},{3,19},{19,3},{4,20},{20... | collective-permute-start | bytes 2457608 | tf_op jit(solution)/shard_map/ppermute | solution.py:576
  6.7 9.1 %collective-permute-start = (f32[135,256]{1,0:T(8,128)S(1)}, f32[135,256]{1,0:T(8,128)S(1)}, u32[]{:S(2)}, u32[]{:S(2)}) collective-permute-start(f32[135,256]{1,0:T(8,128)S(1)} %get-tuple-element.63), channel_id=1, source_target_pairs={{0,4},{4,8},{8,12},{12,0},{16,28},{20,16},{24,20},{28,24},{1,5},{5... | collective-permute-start | bytes 414728 | tf_op jit(solution)/shard_map/ppermute | solution.py:569
  8.3 7.5 %collective-permute-start.1 = (f32[120,256]{1,0:T(8,128)S(1)}, f32[120,256]{1,0:T(8,128)S(1)}, u32[]{:S(2)}, u32[]{:S(2)}) collective-permute-start(f32[120,256]{1,0:T(8,128)S(1)} %get-tuple-element.64), channel_id=1, source_target_pairs={{0,12},{4,0},{8,4},{12,8},{16,20},{20,24},{24,28},{28,16},{1,13},{... | collective-permute-start | bytes 368648 | tf_op jit(solution)/shard_map/ppermute | solution.py:570
  10.5 2.2 %collective-permute-start.2 = (f32[18,8,128]{2,1,0:T(8,128)S(1)}, f32[18,8,128]{2,1,0:T(8,128)S(1)}, u32[]{:S(2)}, u32[]{:S(2)}) collective-permute-start(f32[18,8,128]{2,1,0:T(8,128)S(1)} %get-tuple-element.65), channel_id=1, source_target_pairs={{0,1},{1,2},{2,3},{17,16},{18,17},{19,18},{4,5},{5,6},{6,7},{21,20... | collective-permute-start | bytes 221192 | tf_op jit(solution)/shard_map/ppermute | solution.py:571
  17.6 10.3 %copy-start.8 = (f32[2,5,8,256]{3,2,1,0:T(8,128)}, f32[2,5,8,256]{3,2,1,0:T(8,128)S(1)}, u32[]{:S(2)}) copy-start(f32[2,5,8,256]{3,2,1,0:T(8,128)S(1)} %get-tuple-element.80.keep_ref) | copy-start | bytes 245764
  17.6 14.3 %copy-start.6 = (f32[70,8,256]{2,1,0:T(8,128)}, f32[70,8,256]{2,1,0:T(8,128)S(1)}, u32[]{:S(2)}) copy-start(f32[70,8,256]{2,1,0:T(8,128)S(1)} %get-tuple-element.71.own_ref) | copy-start | bytes 1720324
  17.6 17.9 %collective-permute-start.7 = (f32[70,8,256]{2,1,0:T(8,128)S(1)}, f32[70,8,256]{2,1,0:T(8,128)S(1)}, u32[]{:S(2)}, u32[]{:S(2)}) collective-permute-start(f32[70,8,256]{2,1,0:T(8,128)S(1)} %get-tuple-element.71.own_ref), channel_id=1, source_target_pairs={{0,16},{16,0},{1,17},{17,1},{2,18},{18,2},{3,19},{19,3},{4,20},{20... | collective-permute-start | bytes 1720328 | tf_op jit(solution)/shard_map/ppermute | solution.py:591
  25.7 28.6 %collective-permute-start.8 = (f32[90,8,256]{2,1,0:T(8,128)S(1)}, f32[90,8,256]{2,1,0:T(8,128)S(1)}, u32[]{:S(2)}, u32[]{:S(2)}) collective-permute-start(f32[90,8,256]{2,1,0:T(8,128)S(1)} %get-tuple-element.73.rest_0_.own_ref), channel_id=1, source_target_pairs={{0,16},{16,0},{1,17},{17,1},{2,18},{18,2},{3,19},{19,3},{4,20},{20... | collective-permute-start | bytes 2211848 | tf_op jit(solution)/shard_map/ppermute | solution.py:591
  35.5 18.8 %copy-start.2 = (f32[70,8,256]{2,1,0:T(8,128)}, f32[70,8,256]{2,1,0:T(8,128)S(1)}, u32[]{:S(2)}) copy-start(f32[70,8,256]{2,1,0:T(8,128)S(1)} %collective-permute-done.7.rest_1_.other_ref) | copy-start | bytes 1720324
  37.6 27.8 %copy-start.4 = (f32[80,8,256]{2,1,0:T(8,128)}, f32[80,8,256]{2,1,0:T(8,128)S(1)}, u32[]{:S(2)}) copy-start(f32[80,8,256]{2,1,0:T(8,128)S(1)} %get-tuple-element.75.own_ref) | copy-start | bytes 1966084
  37.6 27.8 %collective-permute-start.9 = (f32[80,8,256]{2,1,0:T(8,128)S(1)}, f32[80,8,256]{2,1,0:T(8,128)S(1)}, u32[]{:S(2)}, u32[]{:S(2)}) collective-permute-start(f32[80,8,256]{2,1,0:T(8,128)S(1)} %get-tuple-element.75.own_ref), channel_id=1, source_target_pairs={{0,16},{16,0},{1,17},{17,1},{2,18},{18,2},{3,19},{19,3},{4,20},{20... | collective-permute-start | bytes 1966088 | tf_op jit(solution)/shard_map/ppermute | solution.py:591
  39.7 14.6 %collective-permute-start.4 = (f32[315,256]{1,0:T(8,128)S(1)}, f32[315,256]{1,0:T(8,128)S(1)}, u32[]{:S(2)}, u32[]{:S(2)}) collective-permute-start(f32[315,256]{1,0:T(8,128)S(1)} %get-tuple-element.68.rest_2_), channel_id=1, source_target_pairs={{0,4},{4,8},{8,12},{12,0},{16,28},{20,16},{24,20},{28,24},{1,5},{5... | collective-permute-start | bytes 967688 | tf_op jit(solution)/shard_map/ppermute | solution.py:569
  41.3 13.0 %collective-permute-start.5 = (f32[280,256]{1,0:T(8,128)S(1)}, f32[280,256]{1,0:T(8,128)S(1)}, u32[]{:S(2)}, u32[]{:S(2)}) collective-permute-start(f32[280,256]{1,0:T(8,128)S(1)} %get-tuple-element.69), channel_id=1, source_target_pairs={{0,12},{4,0},{8,4},{12,8},{16,20},{20,24},{24,28},{28,16},{1,13},{... | collective-permute-start | bytes 860168 | tf_op jit(solution)/shard_map/ppermute | solution.py:570
  43.5 2.2 %collective-permute-start.6 = (f32[18,8,128]{2,1,0:T(8,128)S(1)}, f32[18,8,128]{2,1,0:T(8,128)S(1)}, u32[]{:S(2)}, u32[]{:S(2)}) collective-permute-start(f32[18,8,128]{2,1,0:T(8,128)S(1)} %get-tuple-element.70), channel_id=1, source_target_pairs={{0,1},{1,2},{2,3},{17,16},{18,17},{19,18},{4,5},{5,6},{6,7},{21,20... | collective-permute-start | bytes 221192 | tf_op jit(solution)/shard_map/ppermute | solution.py:571
  58.1 21.4 %collective-permute-start.10 = (f32[80,8,256]{2,1,0:T(8,128)}, f32[80,8,256]{2,1,0:T(8,128)}, u32[]{:S(2)}, u32[]{:S(2)}) collective-permute-start(f32[80,8,256]{2,1,0:T(8,128)} %get-tuple-element.77.own_ref), channel_id=1, source_target_pairs={{0,16},{16,0},{1,17},{17,1},{2,18},{18,2},{3,19},{19,3},{4,20},{20... | collective-permute-start | bytes 1966088 | tf_op jit(solution)/shard_map/ppermute | solution.py:591
  65.4 19.4 %copy-start.11 = (f32[8,256]{1,0:T(8,128)S(1)}, f32[8,256]{1,0:T(8,128)}, u32[]{:S(2)}) copy-start(f32[8,256]{1,0:T(8,128)} %param.11) | copy-start | bytes 24580
  70.2 23.3 %collective-permute-start.12 = (f32[80,8,256]{2,1,0:T(8,128)}, f32[80,8,256]{2,1,0:T(8,128)}, u32[]{:S(2)}, u32[]{:S(2)}) collective-permute-start(f32[80,8,256]{2,1,0:T(8,128)} %get-tuple-element.91.own_ref), channel_id=1, source_target_pairs={{0,16},{16,0},{1,17},{17,1},{2,18},{18,2},{3,19},{19,3},{4,20},{20... | collective-permute-start | bytes 1966088 | tf_op jit(solution)/shard_map/ppermute | solution.py:591
  79.5 18.1 %copy-start.13 = (f32[8,256]{1,0:T(8,128)S(1)}, f32[8,256]{1,0:T(8,128)}, u32[]{:S(2)}) copy-start(f32[8,256]{1,0:T(8,128)} %param.10) | copy-start | bytes 24580
  82.7 25.0 %collective-permute-start.11 = (f32[81,8,256]{2,1,0:T(8,128)S(1)}, f32[81,8,256]{2,1,0:T(8,128)S(1)}, u32[]{:S(2)}, u32[]{:S(2)}) collective-permute-start(f32[81,8,256]{2,1,0:T(8,128)S(1)} %get-tuple-element.79.own_ref), channel_id=1, source_target_pairs={{0,16},{16,0},{1,17},{17,1},{2,18},{18,2},{3,19},{19,3},{4,20},{20... | collective-permute-start | bytes 1990664 | tf_op jit(solution)/shard_map/ppermute | solution.py:591
  93.6 18.1 %copy-start.3 = (f32[70,8,256]{2,1,0:T(8,128)S(1)}, f32[70,8,256]{2,1,0:T(8,128)}, u32[]{:S(2)}) copy-start(f32[70,8,256]{2,1,0:T(8,128)} %copy-done.2) | copy-start | bytes 1720324
  93.6 18.1 %copy-start.7 = (f32[70,8,256]{2,1,0:T(8,128)S(1)}, f32[70,8,256]{2,1,0:T(8,128)}, u32[]{:S(2)}) copy-start(f32[70,8,256]{2,1,0:T(8,128)} %copy-done.6) | copy-start | bytes 1720324
  93.6 18.1 %copy-start.9 = (f32[2,5,8,256]{3,2,1,0:T(8,128)S(1)}, f32[2,5,8,256]{3,2,1,0:T(8,128)}, u32[]{:S(2)}) copy-start(f32[2,5,8,256]{3,2,1,0:T(8,128)} %copy-done.8) | copy-start | bytes 245764
  95.5 26.2 %collective-permute-start.13 = (f32[80,8,256]{2,1,0:T(8,128)S(1)}, f32[80,8,256]{2,1,0:T(8,128)S(1)}, u32[]{:S(2)}, u32[]{:S(2)}) collective-permute-start(f32[80,8,256]{2,1,0:T(8,128)S(1)} %get-tuple-element.98.own_ref), channel_id=1, source_target_pairs={{0,16},{16,0},{1,17},{17,1},{2,18},{18,2},{3,19},{19,3},{4,20},{20... | collective-permute-start | bytes 1966088 | tf_op jit(solution)/shard_map/ppermute | solution.py:591
  109.5 26.3 %collective-permute-start.14 = (f32[80,8,256]{2,1,0:T(8,128)S(1)}, f32[80,8,256]{2,1,0:T(8,128)S(1)}, u32[]{:S(2)}, u32[]{:S(2)}) collective-permute-start(f32[80,8,256]{2,1,0:T(8,128)S(1)} %get-tuple-element.102.own_ref), channel_id=1, source_target_pairs={{0,16},{16,0},{1,17},{17,1},{2,18},{18,2},{3,19},{19,3},{4,20},{20... | collective-permute-start | bytes 1966088 | tf_op jit(solution)/shard_map/ppermute | solution.py:591
  113.5 12.2 %copy-start.1 = (f32[80,8,256]{2,1,0:T(8,128)S(1)}, f32[80,8,256]{2,1,0:T(8,128)}, u32[]{:S(2)}) copy-start(f32[80,8,256]{2,1,0:T(8,128)} %copy-done) | copy-start | bytes 1966084
  113.5 12.2 %copy-start.5 = (f32[80,8,256]{2,1,0:T(8,128)S(1)}, f32[80,8,256]{2,1,0:T(8,128)}, u32[]{:S(2)}) copy-start(f32[80,8,256]{2,1,0:T(8,128)} %copy-done.4) | copy-start | bytes 1966084
  123.6 26.3 %collective-permute-start.15 = (f32[80,8,256]{2,1,0:T(8,128)S(1)}, f32[80,8,256]{2,1,0:T(8,128)S(1)}, u32[]{:S(2)}, u32[]{:S(2)}) collective-permute-start(f32[80,8,256]{2,1,0:T(8,128)S(1)} %get-tuple-element.106.own_ref), channel_id=1, source_target_pairs={{0,16},{16,0},{1,17},{17,1},{2,18},{18,2},{3,19},{19,3},{4,20},{20... | collective-permute-start | bytes 1966088 | tf_op jit(solution)/shard_map/ppermute | solution.py:591
  137.0 19.8 %collective-permute-start.16 = (f32[32,8,256]{2,1,0:T(8,128)S(1)}, f32[32,8,256]{2,1,0:T(8,128)S(1)}, u32[]{:S(2)}, u32[]{:S(2)}) collective-permute-start(f32[32,8,256]{2,1,0:T(8,128)S(1)} %get-tuple-element.110.own_ref), channel_id=1, source_target_pairs={{0,16},{16,0},{1,17},{17,1},{2,18},{18,2},{3,19},{19,3},{4,20},{20... | collective-permute-start | bytes 786440 | tf_op jit(solution)/shard_map/ppermute | solution.py:591
  151.1 10.0 %collective-permute-start.17 = (f32[32,8,256]{2,1,0:T(8,128)S(1)}, f32[32,8,256]{2,1,0:T(8,128)S(1)}, u32[]{:S(2)}, u32[]{:S(2)}) collective-permute-start(f32[32,8,256]{2,1,0:T(8,128)S(1)} %get-tuple-element.114.own_ref), channel_id=1, source_target_pairs={{0,16},{16,0},{1,17},{17,1},{2,18},{18,2},{3,19},{19,3},{4,20},{20... | collective-permute-start | bytes 786440 | tf_op jit(solution)/shard_map/ppermute | solution.py:591
  157.9 5.1 %collective-permute-start.18 = (f32[16,8,256]{2,1,0:T(8,128)S(1)}, f32[16,8,256]{2,1,0:T(8,128)S(1)}, u32[]{:S(2)}, u32[]{:S(2)}) collective-permute-start(f32[16,8,256]{2,1,0:T(8,128)S(1)} %get-tuple-element.118.own_ref), channel_id=1, source_target_pairs={{0,16},{16,0},{1,17},{17,1},{2,18},{18,2},{3,19},{19,3},{4,20},{20... | collective-permute-start | bytes 393224 | tf_op jit(solution)/shard_map/ppermute | solution.py:591
  (1 other events, 0.8 us)
where the time goes:
time: 165 us; the launch traced here: 164 us
  waiting for transfers between devices  70.5 us (43%)
  Pallas kernels  55.9 us (34%)
  starting transfers between devices  36.1 us (22%)
    ppermute x12, waiting for transfers between devices, send(): received.append(lax.ppermute(result[0], 'comp', swap))  53.3 us
    pallas_call x12, Pallas kernels, advect_chunk(): pl.pallas_call(functools.partial(advect_kernel, group, passes, carries, l...  26.3 us
    ppermute x12, starting transfers between devices, send(): received.append(lax.ppermute(result[0], 'comp', swap))  22.9 us
    pallas_call x12, Pallas kernels, source_chunk(): pl.pallas_call(functools.partial(source_kernel, first, count, inner, oute...  22 us
    ppermute x2, waiting for transfers between devices, halo(): lax.ppermute(trail, ('comp', 'tx'), trail_pairs)  11.6 us
    pallas_call x2, Pallas kernels, pack(): pl.pallas_call(functools.partial(pack_kernel, first, count), out_shape=[j...  6.51 us
    ppermute x2, starting transfers between devices, halo(): lax.ppermute(trail, ('comp', 'tx'), trail_pairs)  4.49 us
    ppermute x1, waiting for transfers between devices, paired_shards(): raw = lax.ppermute(raw, 'comp', swap)  3.83 us
  transfers between devices with their start and end apart: 19, of which 15 were waited for; matrix products, arithmetic and copies ran while one was open for 0% of the time, Pallas kernels for 33%

commit v1 on v0

--- a/solution.py
+++ b/solution.py
@@ -219,28 +219,6 @@
     return 2.0 * math.pi * index / NDIR
 
 
-def raw_kernel(spec_ref, raw_ref, sems):
-    copies = []
-    for i, d in enumerate((0, HALF_DIRS - 1)):
-        copy = pltpu.make_async_copy(spec_ref.at[d], raw_ref.at[i], sems.at[i])
-        copy.start()
-        copies.append(copy)
-    for copy in copies:
-        copy.wait()
-
-
-def raw_edges(spec):
-    return pl.pallas_call(
-        raw_kernel,
-        out_shape=jax.ShapeDtypeStruct((2, NFREQ, 8, 256), jnp.float32),
-        in_specs=[pl.BlockSpec(memory_space=pl.ANY)],
-        out_specs=pl.BlockSpec(memory_space=pltpu.VMEM),
-        scratch_shapes=[pltpu.SemaphoreType.DMA((2,))],
-        compiler_params=pltpu.CompilerParams(vmem_limit_bytes=VMEM_BYTES),
-        cost_estimate=SMALL_COST,
-    )(spec)
-
-
 def pack_kernel(first, count, sea_ref, spec_ref, after_ref, lead_ref, trail_ref, lat_ref, held, sems):
     def body(flipped):
         lead_row, trail_row = (0, 7) if flipped else (7, 0)
@@ -248,32 +226,37 @@
         copies = []
         for d in range(HALF_DIRS):
             for h in range(2):
+                place = h * HALF_DIRS + d
                 copy = pltpu.make_async_copy(
-                    spec_ref.at[d, pl.ds(first, count), :, pl.ds(128 * h, 128)], held.at[h * HALF_DIRS + d], sems.at[h * HALF_DIRS + d]
+                    spec_ref.at[pl.ds((d * NFREQ + first) * 8, count * 8), pl.ds(128 * h, 128)],
+                    held.at[pl.ds(place * count * 8, count * 8)],
+                    sems.at[place],
                 )
                 copy.start()
                 copies.append(copy)
-        rows = held.reshape((2 * HALF_DIRS + 1) * count * 8, 128)
         for d in range(HALF_DIRS):
             for h in range(2):
                 copies[2 * d + h].wait()
                 lanes_here = slice(128 * h, 128 * h + 128)
                 start = (h * HALF_DIRS + d) * count * 8
                 if d < LEAD_DIRS:
-                    column = rows[pl.ds(start + lead_row, count, stride=8), :]
+                    column = held[pl.ds(start + lead_row, count, stride=8), :]
                     lead_ref[d * count : (d + 1) * count, lanes_here] = column * sea_ref[lead_row : lead_row + 1, lanes_here]
                 elif d > LEAD_DIRS:
                     t = d - LEAD_DIRS - 1
-                    column = rows[pl.ds(start + trail_row, count, stride=8), :]
+                    column = held[pl.ds(start + trail_row, count, stride=8), :]
                     trail_ref[t * count : (t + 1) * count, lanes_here] = column * sea_ref[trail_row : trail_row + 1, lanes_here]
         lane = 0 if flipped else 127
         lanes = lax.broadcasted_iota(jnp.int32, (8, 128), 1)
         sea_line = jnp.broadcast_to(sea_ref[:, 128 * part + lane : 128 * part + lane + 1], (8, 128))
 
+        def slab(d, f):
+            return held[pl.ds(pl.multiple_of((part * HALF_DIRS + d) * count * 8 + f * 8, 8), 8), :]
+
         def one(f, kept):
             here = lanes == f
             return tuple(
-                jnp.where(here, jnp.broadcast_to(held[part * HALF_DIRS + d, f][:, lane : lane + 1], (8, 128)), kept[d])
+                jnp.where(here, jnp.broadcast_to(slab(d, f)[:, lane : lane + 1], (8, 128)), kept[d])
                 for d in range(HALF_DIRS)
             )
 
@@ -306,7 +289,7 @@
         in_specs=[vmem, hold, hold],
         out_specs=[vmem] * 3,
         scratch_shapes=[
-            pltpu.VMEM((2 * HALF_DIRS + 1, count, 8, 128), jnp.float32),
+            pltpu.VMEM(((2 * HALF_DIRS + 1) * count * 8, 128), jnp.float32),
             pltpu.SemaphoreType.DMA((2 * HALF_DIRS,)),
         ],
         compiler_params=pltpu.CompilerParams(vmem_limit_bytes=VMEM_BYTES),
@@ -332,7 +315,7 @@
     sea_ref, slope_ref, spec_ref, lead_ref, trail_ref, lat_ref, steep_ref, *rest,
 ):
     sums = any(summed for *_, summed in passes)
-    raw_ref = rest[0] if has_raw else None
+    raw_refs = rest[:has_raw]
     rest = rest[has_raw + waits :]
     held, turn, sem = rest[-3:]
     send_ref, keep_ref = rest[:2]
@@ -369,9 +352,9 @@
 
             def energy(d):
                 if d < 0:
-                    return raw_ref[1, first + f] * sea
+                    return raw_refs[1][first + f] * sea
                 if d >= HALF_DIRS:
-                    return raw_ref[0, first + f] * sea
+                    return raw_refs[0][first + f] * sea
                 return held[d, base + f] * sea
 
             known = {}
@@ -434,7 +417,6 @@
     vmem = pl.BlockSpec(memory_space=pltpu.VMEM)
     hold = pl.BlockSpec(memory_space=pl.ANY)
     slabs = sum(count * len(place) for _, count, _, place, _ in passes if place is not None)
-    raw = () if raw is None else (raw,)
     out_shape = [
         jax.ShapeDtypeStruct((slabs + carries, 8, 256), jnp.float32),
         jax.ShapeDtypeStruct((HALF_DIRS - 2 * SIDE_DIRS, passes[0][1], 8, 256), jnp.float32),
@@ -558,13 +540,14 @@
     trail_pairs = joined(tiles_x, -1, True)
     lat_pairs = joined(tiles_y, 1, False)
 
+    rows = pltpu.with_memory_space_constraint(spectrum.reshape(HALF_DIRS * NFREQ * 8, 256), pltpu.HBM)
     spec = pltpu.with_memory_space_constraint(spec, pltpu.HBM)
     bounds = chunk_bounds()
-    raw = raw_edges(spec)
+    edges = [lax.slice_in_dim(spectrum, d * NFREQ, (d + 1) * NFREQ) for d in OUTER_DIRS]
 
     def halo(g, after):
         begin, end = HALO_GROUPS[g]
-        lead, trail, lat = pack(begin, end - begin, sea, spec, after)
+        lead, trail, lat = pack(begin, end - begin, sea, rows, after)
         sides = (
             lax.ppermute(lead, ("comp", "tx"), lead_pairs),
             lax.ppermute(trail, ("comp", "tx"), trail_pairs),
@@ -572,8 +555,8 @@
         )
         return sides, lead
 
-    first_sides, _ = halo(0, raw)
-    raw = lax.ppermute(raw, "comp", swap)
+    first_sides, _ = halo(0, edges[1])
+    raw = tuple(lax.ppermute(edge, "comp", swap) for edge in edges)
     early = sum(end <= HALO_GROUPS[0][1] for _, end in bounds)
     counts = [end - begin for begin, end in bounds]
     places = [slab_index(INNER_DIRS if i == 0 else ALL_DIRS, counts[i]) for i in range(len(bounds))]
@@ -607,7 +590,7 @@
             passes.append((bounds[0][0], counts[0], OUTER_DIRS, edge_place, True))
         if i >= 2:
             after = (received[i - 2], packed)
-        result = advect(passes, first_sides, False, steep, raw if i else None, after)
+        result = advect(passes, first_sides, False, steep, raw if i else (), after)
         send(result)
         steep = result[2]
         if i == 1:

time: 165 us -> 167 us (1.012)
  waiting for transfers between devices: 70.5 us -> 82.4 us
  starting transfers between devices: 36.1 us -> 24.8 us
    ppermute x12, starting transfers between devices: 22.9 us -> 8.66 us  [send(): received.append(lax.ppermute(result[0], 'comp', swap))]
    ppermute x12, waiting for transfers between devices: 53.3 us -> 65.3 us  [send(): received.append(lax.ppermute(result[0], 'comp', swap))]
    ppermute x1 -> x2, starting transfers between devices: 3 us -> 3.38 us  [paired_shards(): raw = tuple((lax.ppermute(edge, 'comp', swap) for edge in edges))]
    ppermute x1 -> x2, waiting for transfers between devices: 3.83 us -> 3.49 us  [paired_shards(): raw = tuple((lax.ppermute(edge, 'comp', swap) for edge in edges))]
  transfers between devices with their start and end apart: 19 -> 20, of which waited for: 15 -> 16; matrix products, arithmetic and copies ran while one was open for 0% -> 0% of each run, Pallas kernels for 33% -> 33%
where the time goes in v1:
time: 167 us; the launch traced here: 165 us
  waiting for transfers between devices  82.4 us (49%)
  Pallas kernels  54.7 us (33%)
  starting transfers between devices  24.8 us (15%)
  local copies, waits for them, and re-layouts  2.14 us (1%)
    ppermute x12, waiting for transfers between devices, send(): received.append(lax.ppermute(result[0], 'comp', swap))  65.3 us
    pallas_call x12, Pallas kernels, advect_chunk(): pl.pallas_call(functools.partial(advect_kernel, group, passes, carries, l...  26.2 us
    pallas_call x12, Pallas kernels, source_chunk(): pl.pallas_call(functools.partial(source_kernel, first, count, inner, oute...  22 us
    ppermute x2, waiting for transfers between devices, halo(): lax.ppermute(trail, ('comp', 'tx'), trail_pairs)  12.2 us
    ppermute x12, starting transfers between devices, send(): received.append(lax.ppermute(result[0], 'comp', swap))  8.66 us
    pallas_call x2, Pallas kernels, pack(): pl.pallas_call(functools.partial(pack_kernel, first, count), out_shape=[j...  6.51 us
    ppermute x2, starting transfers between devices, halo(): lax.ppermute(trail, ('comp', 'tx'), trail_pairs)  6 us
    ppermute x2, starting transfers between devices, halo(): lax.ppermute(lat, ('comp', 'ty'), lat_pairs)  3.97 us
  transfers between devices with their start and end apart: 20, of which 16 were waited for; matrix products, arithmetic and copies ran while one was open for 0% of the time, Pallas kernels for 33%

profile of v1, /device:TPU:0, one launch (start us, length us, event | category | flops | bytes accessed | tf_op | source)
XLA Modules:
  0.0 165.1 jit_solution(4331423452503158828)
XLA Ops:
  1.2 3.0 %collective-permute-start.4 = (f32[50,8,256]{2,1,0:T(8,128)S(1)}, f32[50,8,256]{2,1,0:T(8,128)S(1)}, u32[]{:S(2)}, u32[]{:S(2)}) collective-permute-start(f32[50,8,256]{2,1,0:T(8,128)S(1)} %get-tuple-element.122.after_ref), channel_id=1, source_target_pairs={{0,16},{16,0},{1,17},{17,1},{2,18},{18,2},{3,19},{19,3},{4,20},{20... | collective-permute-start | bytes 1228808 | tf_op jit(solution)/shard_map/ppermute | solution.py:559
  4.9 2.5 %shard_map.55 = (f32[135,256]{1,0:T(8,128)S(1)}, f32[120,256]{1,0:T(8,128)S(1)}, f32[18,8,128]{2,1,0:T(8,128)S(1)}) custom-call(f32[8,256]{1,0:T(8,128)S(1)} %convert_element_type.7.sea_ref, f32[7200,256]{1,0:T(8,128)} %bitcast.9, f32[50,8,256]{2,1,0:T(8,128)S(1)} %get-tuple-element.122.after_ref), custom_call_target="tpu_custom_call" | custom-call | flops 1024 | bytes 1024 | tf_op jit(solution)/shard_map/pallas_call | solution.py:282
  9.0 2.2 %collective-permute-start.1 = (f32[120,256]{1,0:T(8,128)S(1)}, f32[120,256]{1,0:T(8,128)S(1)}, u32[]{:S(2)}, u32[]{:S(2)}) collective-permute-start(f32[120,256]{1,0:T(8,128)S(1)} %get-tuple-element.64), channel_id=1, source_target_pairs={{0,12},{4,0},{8,4},{12,8},{16,20},{20,24},{24,28},{28,16},{1,13},{... | collective-permute-start | bytes 368648 | tf_op jit(solution)/shard_map/ppermute | solution.py:553
  13.4 3.1 %collective-permute-done.1.trail_ref = f32[120,256]{1,0:T(8,128)S(1)} collective-permute-done((f32[120,256]{1,0:T(8,128)S(1)}, f32[120,256]{1,0:T(8,128)S(1)}, u32[]{:S(2)}, u32[]{:S(2)}) %collective-permute-start.1) | collective-permute-done | bytes 122912 | tf_op jit(solution)/shard_map/ppermute | solution.py:553
  18.3 1.8 %collective-permute-start.8 = (f32[70,8,256]{2,1,0:T(8,128)S(1)}, f32[70,8,256]{2,1,0:T(8,128)S(1)}, u32[]{:S(2)}, u32[]{:S(2)}) collective-permute-start(f32[70,8,256]{2,1,0:T(8,128)S(1)} %get-tuple-element.71.own_ref), channel_id=1, source_target_pairs={{0,16},{16,0},{1,17},{17,1},{2,18},{18,2},{3,19},{19,3},{4,20},{20... | collective-permute-start | bytes 1720328 | tf_op jit(solution)/shard_map/ppermute | solution.py:574
  20.1 3.5 %collective-permute-done.3.rest_0_ = f32[50,8,256]{2,1,0:T(8,128)S(1)} collective-permute-done((f32[50,8,256]{2,1,0:T(8,128)S(1)}, f32[50,8,256]{2,1,0:T(8,128)S(1)}, u32[]{:S(2)}, u32[]{:S(2)}) %collective-permute-start.3) | collective-permute-done | bytes 409632 | tf_op jit(solution)/shard_map/ppermute | solution.py:559
  23.6 2.5 %shard_map.57 = (f32[90,8,256]{2,1,0:T(8,128)S(1)}, f32[2,5,8,256]{3,2,1,0:T(8,128)S(1)}, f32[8,256]{1,0:T(8,128)S(1)}) custom-call(f32[8,256]{1,0:T(8,128)S(1)} %convert_element_type.7.sea_ref, f32[2,8,256]{2,1,0:T(8,128)S(1)} %broadcast_multiply_fusion.slope_ref, f32[18,50,8,256]{3,2,1,0:T(8,128)} %bitcast.11, ...), custom_call_target="tpu_custom_call" | custom-call | flops 1024 | bytes 1024 | tf_op jit(solution)/shard_map/pallas_call | solution.py:426
  26.5 4.1 %shard_map.58 = (f32[315,256]{1,0:T(8,128)S(1)}, f32[280,256]{1,0:T(8,128)S(1)}, f32[18,8,128]{2,1,0:T(8,128)S(1)}) custom-call(f32[8,256]{1,0:T(8,128)S(1)} %convert_element_type.7.sea_ref, f32[7200,256]{1,0:T(8,128)} %bitcast.12, f32[8,256]{1,0:T(8,128)S(1)} %get-tuple-element.67.after_ref.steep_ref), custom_call_target="tpu_custom_call" | custom-call | flops 1024 | bytes 1024 | tf_op jit(solution)/shard_map/pallas_call | solution.py:282
  30.6 5.3 %collective-permute-done.8.rest_2_.other_ref = f32[70,8,256]{2,1,0:T(8,128)S(1)} collective-permute-done((f32[70,8,256]{2,1,0:T(8,128)S(1)}, f32[70,8,256]{2,1,0:T(8,128)S(1)}, u32[]{:S(2)}, u32[]{:S(2)}) %collective-permute-start.8) | collective-permute-done | bytes 573472 | tf_op jit(solution)/shard_map/ppermute | solution.py:574
  35.9 2.0 %shard_map.59 = (f32[80,8,256]{2,1,0:T(8,128)S(1)}, f32[2,5,8,256]{3,2,1,0:T(8,128)S(1)}, f32[8,256]{1,0:T(8,128)S(1)}) custom-call(f32[8,256]{1,0:T(8,128)S(1)} %convert_element_type.7.sea_ref, f32[2,8,256]{2,1,0:T(8,128)S(1)} %broadcast_multiply_fusion.slope_ref, f32[18,50,8,256]{3,2,1,0:T(8,128)} %bitcast.13, ...), custom_call_target="tpu_custom_call" | custom-call | flops 1024 | bytes 1024 | tf_op jit(solution)/shard_map/pallas_call | solution.py:426
  39.6 3.7 %collective-permute-start.6 = (f32[280,256]{1,0:T(8,128)S(1)}, f32[280,256]{1,0:T(8,128)S(1)}, u32[]{:S(2)}, u32[]{:S(2)}) collective-permute-start(f32[280,256]{1,0:T(8,128)S(1)} %get-tuple-element.69), channel_id=1, source_target_pairs={{0,12},{4,0},{8,4},{12,8},{16,20},{20,24},{24,28},{28,16},{1,13},{... | collective-permute-start | bytes 860168 | tf_op jit(solution)/shard_map/ppermute | solution.py:553
  43.3 2.7 %collective-permute-start.7 = (f32[18,8,128]{2,1,0:T(8,128)S(1)}, f32[18,8,128]{2,1,0:T(8,128)S(1)}, u32[]{:S(2)}, u32[]{:S(2)}) collective-permute-start(f32[18,8,128]{2,1,0:T(8,128)S(1)} %get-tuple-element.70), channel_id=1, source_target_pairs={{0,1},{1,2},{2,3},{17,16},{18,17},{19,18},{4,5},{5,6},{6,7},{21,20... | collective-permute-start | bytes 221192 | tf_op jit(solution)/shard_map/ppermute | solution.py:554
  46.9 9.1 %collective-permute-done.6.trail_ref = f32[280,256]{1,0:T(8,128)S(1)} collective-permute-done((f32[280,256]{1,0:T(8,128)S(1)}, f32[280,256]{1,0:T(8,128)S(1)}, u32[]{:S(2)}, u32[]{:S(2)}) %collective-permute-start.6) | collective-permute-done | bytes 286752 | tf_op jit(solution)/shard_map/ppermute | solution.py:553
  56.0 3.8 %shard_map.60 = (f32[80,8,256]{2,1,0:T(8,128)}, f32[2,5,8,256]{3,2,1,0:T(8,128)S(1)}, f32[8,256]{1,0:T(8,128)S(1)}) custom-call(f32[8,256]{1,0:T(8,128)S(1)} %convert_element_type.7.sea_ref, f32[2,8,256]{2,1,0:T(8,128)S(1)} %broadcast_multiply_fusion.slope_ref, f32[18,50,8,256]{3,2,1,0:T(8,128)} %bitcast.14, f32[315,256]{1,0:T(8,128)S(1)} %collective-permute-done.5.lead_ref, ...), custom_call_target="tpu_custom_call" | custom-call | flops 1024 | bytes 1024 | tf_op jit(solution)/shard_map/pallas_call | solution.py:426
  59.8 1.8 %collective-permute-start.11 = (f32[80,8,256]{2,1,0:T(8,128)}, f32[80,8,256]{2,1,0:T(8,128)}, u32[]{:S(2)}, u32[]{:S(2)}) collective-permute-start(f32[80,8,256]{2,1,0:T(8,128)} %get-tuple-element.77.own_ref), channel_id=1, source_target_pairs={{0,16},{16,0},{1,17},{17,1},{2,18},{18,2},{3,19},{19,3},{4,20},{20... | collective-permute-start | bytes 1966088 | tf_op jit(solution)/shard_map/ppermute | solution.py:574
  61.6 4.1 %collective-permute-done.10.rest_2_.other_ref = f32[80,8,256]{2,1,0:T(8,128)S(1)} collective-permute-done((f32[80,8,256]{2,1,0:T(8,128)S(1)}, f32[80,8,256]{2,1,0:T(8,128)S(1)}, u32[]{:S(2)}, u32[]{:S(2)}) %collective-permute-start.10) | collective-permute-done | bytes 655392 | tf_op jit(solution)/shard_map/ppermute | solution.py:574
  65.8 4.0 %shard_map.61 = (f32[80,8,256]{2,1,0:T(8,128)}, f32[2,5,8,256]{3,2,1,0:T(8,128)S(1)}, f32[8,256]{1,0:T(8,128)S(1)}) custom-call(f32[8,256]{1,0:T(8,128)S(1)} %convert_element_type.7.sea_ref, f32[2,8,256]{2,1,0:T(8,128)S(1)} %broadcast_multiply_fusion.slope_ref, f32[18,50,8,256]{3,2,1,0:T(8,128)} %bitcast.15, f32[315,256]{1,0:T(8,128)S(1)} %collective-permute-done.5.lead_ref, ...), custom_call_target="tpu_custom_call" | custom-call | flops 1024 | bytes 1024 | tf_op jit(solution)/shard_map/pallas_call | solution.py:426
  70.9 9.0 %collective-permute-done.11.rest_2_.other_ref = f32[80,8,256]{2,1,0:T(8,128)} collective-permute-done((f32[80,8,256]{2,1,0:T(8,128)}, f32[80,8,256]{2,1,0:T(8,128)}, u32[]{:S(2)}, u32[]{:S(2)}) %collective-permute-start.11) | collective-permute-done | bytes 655392 | tf_op jit(solution)/shard_map/ppermute | solution.py:574
  79.9 3.1 %shard_map.62 = (f32[81,8,256]{2,1,0:T(8,128)S(1)}, f32[2,5,8,256]{3,2,1,0:T(8,128)S(1)}, f32[8,256]{1,0:T(8,128)S(1)}) custom-call(f32[8,256]{1,0:T(8,128)S(1)} %convert_element_type.7.sea_ref, f32[2,8,256]{2,1,0:T(8,128)S(1)} %broadcast_multiply_fusion.slope_ref, f32[18,50,8,256]{3,2,1,0:T(8,128)} %bitcast.16, ...), custom_call_target="tpu_custom_call" | custom-call | flops 1024 | bytes 1024 | tf_op jit(solution)/shard_map/pallas_call | solution.py:426
  83.5 10.4 %collective-permute-done.13.other_ref.rest_2_ = f32[80,8,256]{2,1,0:T(8,128)} collective-permute-done((f32[80,8,256]{2,1,0:T(8,128)}, f32[80,8,256]{2,1,0:T(8,128)}, u32[]{:S(2)}, u32[]{:S(2)}) %collective-permute-start.13) | collective-permute-done | bytes 655392 | tf_op jit(solution)/shard_map/ppermute | solution.py:574
  94.0 1.9 %shard_map.69 = (f32[80,8,256]{2,1,0:T(8,128)S(1)}, f32[2,5,8,256]{3,2,1,0:T(8,128)S(1)}) custom-call(f32[8,256]{1,0:T(8,128)S(1)} %convert_element_type.7.sea_ref, f32[2,8,256]{2,1,0:T(8,128)S(1)} %broadcast_multiply_fusion.slope_ref, f32[18,50,8,256]{3,2,1,0:T(8,128)} %bitcast.17, f32[315,256]{1,0:T(8,128)S(1)} %collective-permute-done.5.lead_ref, ...), custom_call_target="tpu_custom_call" | custom-call | flops 1024 | bytes 1024 | tf_op jit(solution)/shard_map/pallas_call | solution.py:426
  96.3 11.8 %collective-permute-done.12.other_ref.rest_2_ = f32[81,8,256]{2,1,0:T(8,128)S(1)} collective-permute-done((f32[81,8,256]{2,1,0:T(8,128)S(1)}, f32[81,8,256]{2,1,0:T(8,128)S(1)}, u32[]{:S(2)}, u32[]{:S(2)}) %collective-permute-start.12) | collective-permute-done | bytes 663584 | tf_op jit(solution)/shard_map/ppermute | solution.py:574
  112.2 1.8 %shard_map.64 = (f32[18,50,8,256]{3,2,1,0:T(8,128)}, f32[18,8,256]{2,1,0:T(8,128)S(1)}) custom-call(f32[2,8,256]{2,1,0:T(8,128)S(1)} %maximum_multiply_fusion.wind_ref, f32[8,256]{1,0:T(8,128)S(1)} %get-tuple-element.78.steep_a_ref.steep_ref, f32[8,256]{1,0:T(8,128)S(1)} %slice_bitcast_fusion.steep_b_ref, ...), custom_call_target="tpu_custom_call", output_to_operand_aliasing={{0}: (7, {})} | custom-call | flops 1024 | bytes 1024 | tf_op jit(solution)/shard_map/pallas_call | solution.py:502
  114.0 8.1 %collective-permute-done.14.other_ref.rest_2_ = f32[80,8,256]{2,1,0:T(8,128)S(1)} collective-permute-done((f32[80,8,256]{2,1,0:T(8,128)S(1)}, f32[80,8,256]{2,1,0:T(8,128)S(1)}, u32[]{:S(2)}, u32[]{:S(2)}) %collective-permute-start.14) | collective-permute-done | bytes 655392 | tf_op jit(solution)/shard_map/ppermute | solution.py:574
  126.1 3.1 %shard_map.66 = (f32[18,50,8,256]{3,2,1,0:T(8,128)}, f32[18,8,256]{2,1,0:T(8,128)S(1)}) custom-call(f32[2,8,256]{2,1,0:T(8,128)S(1)} %maximum_multiply_fusion.wind_ref, f32[8,256]{1,0:T(8,128)S(1)} %get-tuple-element.78.steep_a_ref.steep_ref, f32[8,256]{1,0:T(8,128)S(1)} %slice_bitcast_fusion.steep_b_ref, ...), custom_call_target="tpu_custom_call", output_to_operand_aliasing={{0}: (7, {})} | custom-call | flops 1024 | bytes 1024 | tf_op jit(solution)/shard_map/pallas_call | solution.py:502
  129.2 3.1 %shard_map.67 = (f32[18,50,8,256]{3,2,1,0:T(8,128)}, f32[18,8,256]{2,1,0:T(8,128)S(1)}) custom-call(f32[2,8,256]{2,1,0:T(8,128)S(1)} %maximum_multiply_fusion.wind_ref, f32[8,256]{1,0:T(8,128)S(1)} %get-tuple-element.78.steep_a_ref.steep_ref, f32[8,256]{1,0:T(8,128)S(1)} %slice_bitcast_fusion.steep_b_ref, ...), custom_call_target="tpu_custom_call", output_to_operand_aliasing={{0}: (7, {})} | custom-call | flops 1024 | bytes 1024 | tf_op jit(solution)/shard_map/pallas_call | solution.py:502
  132.3 3.8 %collective-permute-done.15.other_ref.rest_2_ = f32[80,8,256]{2,1,0:T(8,128)S(1)} collective-permute-done((f32[80,8,256]{2,1,0:T(8,128)S(1)}, f32[80,8,256]{2,1,0:T(8,128)S(1)}, u32[]{:S(2)}, u32[]{:S(2)}) %collective-permute-start.15) | collective-permute-done | bytes 655392 | tf_op jit(solution)/shard_map/ppermute | solution.py:574
  137.8 1.8 %shard_map.68 = (f32[18,50,8,256]{3,2,1,0:T(8,128)}, f32[18,8,256]{2,1,0:T(8,128)S(1)}) custom-call(f32[2,8,256]{2,1,0:T(8,128)S(1)} %maximum_multiply_fusion.wind_ref, f32[8,256]{1,0:T(8,128)S(1)} %get-tuple-element.78.steep_a_ref.steep_ref, f32[8,256]{1,0:T(8,128)S(1)} %slice_bitcast_fusion.steep_b_ref, ...), custom_call_target="tpu_custom_call", output_to_operand_aliasing={{0}: (7, {})} | custom-call | flops 1024 | bytes 1024 | tf_op jit(solution)/shard_map/pallas_call | solution.py:502
  139.6 1.8 %shard_map.70 = (f32[18,50,8,256]{3,2,1,0:T(8,128)}, f32[18,8,256]{2,1,0:T(8,128)S(1)}) custom-call(f32[2,8,256]{2,1,0:T(8,128)S(1)} %maximum_multiply_fusion.wind_ref, f32[8,256]{1,0:T(8,128)S(1)} %get-tuple-element.78.steep_a_ref.steep_ref, f32[8,256]{1,0:T(8,128)S(1)} %slice_bitcast_fusion.steep_b_ref, ...), custom_call_target="tpu_custom_call", output_to_operand_aliasing={{0}: (7, {})} | custom-call | flops 1024 | bytes 1024 | tf_op jit(solution)/shard_map/pallas_call | solution.py:502
  141.5 8.7 %collective-permute-done.16.other_ref.rest_2_ = f32[80,8,256]{2,1,0:T(8,128)S(1)} collective-permute-done((f32[80,8,256]{2,1,0:T(8,128)S(1)}, f32[80,8,256]{2,1,0:T(8,128)S(1)}, u32[]{:S(2)}, u32[]{:S(2)}) %collective-permute-start.16) | collective-permute-done | bytes 655392 | tf_op jit(solution)/shard_map/ppermute | solution.py:574
  153.7 1.8 %shard_map.74 = (f32[18,50,8,256]{3,2,1,0:T(8,128)}, f32[18,8,256]{2,1,0:T(8,128)S(1)}) custom-call(f32[2,8,256]{2,1,0:T(8,128)S(1)} %maximum_multiply_fusion.wind_ref, f32[8,256]{1,0:T(8,128)S(1)} %get-tuple-element.78.steep_a_ref.steep_ref, f32[8,256]{1,0:T(8,128)S(1)} %slice_bitcast_fusion.steep_b_ref, ...), custom_call_target="tpu_custom_call", output_to_operand_aliasing={{0}: (7, {})} | custom-call | flops 1024 | bytes 1024 | tf_op jit(solution)/shard_map/pallas_call | solution.py:502
  159.4 2.0 %collective-permute-done.18.other_ref = f32[32,8,256]{2,1,0:T(8,128)S(1)} collective-permute-done((f32[32,8,256]{2,1,0:T(8,128)S(1)}, f32[32,8,256]{2,1,0:T(8,128)S(1)}, u32[]{:S(2)}, u32[]{:S(2)}) %collective-permute-start.18) | collective-permute-done | bytes 262176 | tf_op jit(solution)/shard_map/ppermute | solution.py:574
  (69 shorter events, 33.3 us)
Async XLA Ops:
  0.0 12.9 %copy-start.10 = (f32[2,8,256]{2,1,0:T(8,128)S(1)}, f32[2,8,256]{2,1,0:T(8,128)}, u32[]{:S(2)}) copy-start(f32[2,8,256]{2,1,0:T(8,128)} %param.9) | copy-start | bytes 49156
  1.2 18.9 %collective-permute-start.4 = (f32[50,8,256]{2,1,0:T(8,128)S(1)}, f32[50,8,256]{2,1,0:T(8,128)S(1)}, u32[]{:S(2)}, u32[]{:S(2)}) collective-permute-start(f32[50,8,256]{2,1,0:T(8,128)S(1)} %get-tuple-element.122.after_ref), channel_id=1, source_target_pairs={{0,16},{16,0},{1,17},{17,1},{2,18},{18,2},{3,19},{19,3},{4,20},{20... | collective-permute-start | bytes 1228808 | tf_op jit(solution)/shard_map/ppermute | solution.py:559
  7.4 9.1 %collective-permute-start = (f32[135,256]{1,0:T(8,128)S(1)}, f32[135,256]{1,0:T(8,128)S(1)}, u32[]{:S(2)}, u32[]{:S(2)}) collective-permute-start(f32[135,256]{1,0:T(8,128)S(1)} %get-tuple-element.63), channel_id=1, source_target_pairs={{0,4},{4,8},{8,12},{12,0},{16,28},{20,16},{24,20},{28,24},{1,5},{5... | collective-permute-start | bytes 414728 | tf_op jit(solution)/shard_map/ppermute | solution.py:552
  9.0 7.5 %collective-permute-start.1 = (f32[120,256]{1,0:T(8,128)S(1)}, f32[120,256]{1,0:T(8,128)S(1)}, u32[]{:S(2)}, u32[]{:S(2)}) collective-permute-start(f32[120,256]{1,0:T(8,128)S(1)} %get-tuple-element.64), channel_id=1, source_target_pairs={{0,12},{4,0},{8,4},{12,8},{16,20},{20,24},{24,28},{28,16},{1,13},{... | collective-permute-start | bytes 368648 | tf_op jit(solution)/shard_map/ppermute | solution.py:553
  11.2 2.2 %collective-permute-start.2 = (f32[18,8,128]{2,1,0:T(8,128)S(1)}, f32[18,8,128]{2,1,0:T(8,128)S(1)}, u32[]{:S(2)}, u32[]{:S(2)}) collective-permute-start(f32[18,8,128]{2,1,0:T(8,128)S(1)} %get-tuple-element.65), channel_id=1, source_target_pairs={{0,1},{1,2},{2,3},{17,16},{18,17},{19,18},{4,5},{5,6},{6,7},{21,20... | collective-permute-start | bytes 221192 | tf_op jit(solution)/shard_map/ppermute | solution.py:554
  12.5 11.1 %collective-permute-start.3 = (f32[50,8,256]{2,1,0:T(8,128)S(1)}, f32[50,8,256]{2,1,0:T(8,128)S(1)}, u32[]{:S(2)}, u32[]{:S(2)}) collective-permute-start(f32[50,8,256]{2,1,0:T(8,128)S(1)} %get-tuple-element.121), channel_id=1, source_target_pairs={{0,16},{16,0},{1,17},{17,1},{2,18},{18,2},{3,19},{19,3},{4,20},{20... | collective-permute-start | bytes 1228808 | tf_op jit(solution)/shard_map/ppermute | solution.py:559
  18.3 8.2 %copy-start.8 = (f32[2,5,8,256]{3,2,1,0:T(8,128)}, f32[2,5,8,256]{3,2,1,0:T(8,128)S(1)}, u32[]{:S(2)}) copy-start(f32[2,5,8,256]{3,2,1,0:T(8,128)S(1)} %get-tuple-element.80.keep_ref) | copy-start | bytes 245764
  18.3 12.3 %copy-start.6 = (f32[70,8,256]{2,1,0:T(8,128)}, f32[70,8,256]{2,1,0:T(8,128)S(1)}, u32[]{:S(2)}) copy-start(f32[70,8,256]{2,1,0:T(8,128)S(1)} %get-tuple-element.71.own_ref) | copy-start | bytes 1720324
  18.3 17.6 %collective-permute-start.8 = (f32[70,8,256]{2,1,0:T(8,128)S(1)}, f32[70,8,256]{2,1,0:T(8,128)S(1)}, u32[]{:S(2)}, u32[]{:S(2)}) collective-permute-start(f32[70,8,256]{2,1,0:T(8,128)S(1)} %get-tuple-element.71.own_ref), channel_id=1, source_target_pairs={{0,16},{16,0},{1,17},{17,1},{2,18},{18,2},{3,19},{19,3},{4,20},{20... | collective-permute-start | bytes 1720328 | tf_op jit(solution)/shard_map/ppermute | solution.py:574
  26.1 29.9 %collective-permute-start.9 = (f32[90,8,256]{2,1,0:T(8,128)S(1)}, f32[90,8,256]{2,1,0:T(8,128)S(1)}, u32[]{:S(2)}, u32[]{:S(2)}) collective-permute-start(f32[90,8,256]{2,1,0:T(8,128)S(1)} %get-tuple-element.73.rest_0_.own_ref), channel_id=1, source_target_pairs={{0,16},{16,0},{1,17},{17,1},{2,18},{18,2},{3,19},{19,3},{4,20},{20... | collective-permute-start | bytes 2211848 | tf_op jit(solution)/shard_map/ppermute | solution.py:574
  35.9 2.0 %copy-start.2 = (f32[70,8,256]{2,1,0:T(8,128)}, f32[70,8,256]{2,1,0:T(8,128)S(1)}, u32[]{:S(2)}) copy-start(f32[70,8,256]{2,1,0:T(8,128)S(1)} %collective-permute-done.8.rest_2_.other_ref) | copy-start | bytes 1720324
  37.9 27.8 %copy-start.4 = (f32[80,8,256]{2,1,0:T(8,128)}, f32[80,8,256]{2,1,0:T(8,128)S(1)}, u32[]{:S(2)}) copy-start(f32[80,8,256]{2,1,0:T(8,128)S(1)} %get-tuple-element.75.own_ref) | copy-start | bytes 1966084
  38.0 27.8 %collective-permute-start.10 = (f32[80,8,256]{2,1,0:T(8,128)S(1)}, f32[80,8,256]{2,1,0:T(8,128)S(1)}, u32[]{:S(2)}, u32[]{:S(2)}) collective-permute-start(f32[80,8,256]{2,1,0:T(8,128)S(1)} %get-tuple-element.75.own_ref), channel_id=1, source_target_pairs={{0,16},{16,0},{1,17},{17,1},{2,18},{18,2},{3,19},{19,3},{4,20},{20... | collective-permute-start | bytes 1966088 | tf_op jit(solution)/shard_map/ppermute | solution.py:574
  38.4 17.6 %collective-permute-start.5 = (f32[315,256]{1,0:T(8,128)S(1)}, f32[315,256]{1,0:T(8,128)S(1)}, u32[]{:S(2)}, u32[]{:S(2)}) collective-permute-start(f32[315,256]{1,0:T(8,128)S(1)} %get-tuple-element.68.rest_3_), channel_id=1, source_target_pairs={{0,4},{4,8},{8,12},{12,0},{16,28},{20,16},{24,20},{28,24},{1,5},{5... | collective-permute-start | bytes 967688 | tf_op jit(solution)/shard_map/ppermute | solution.py:552
  39.6 16.4 %collective-permute-start.6 = (f32[280,256]{1,0:T(8,128)S(1)}, f32[280,256]{1,0:T(8,128)S(1)}, u32[]{:S(2)}, u32[]{:S(2)}) collective-permute-start(f32[280,256]{1,0:T(8,128)S(1)} %get-tuple-element.69), channel_id=1, source_target_pairs={{0,12},{4,0},{8,4},{12,8},{16,20},{20,24},{24,28},{28,16},{1,13},{... | collective-permute-start | bytes 860168 | tf_op jit(solution)/shard_map/ppermute | solution.py:553
  43.3 3.6 %collective-permute-start.7 = (f32[18,8,128]{2,1,0:T(8,128)S(1)}, f32[18,8,128]{2,1,0:T(8,128)S(1)}, u32[]{:S(2)}, u32[]{:S(2)}) collective-permute-start(f32[18,8,128]{2,1,0:T(8,128)S(1)} %get-tuple-element.70), channel_id=1, source_target_pairs={{0,1},{1,2},{2,3},{17,16},{18,17},{19,18},{4,5},{5,6},{6,7},{21,20... | collective-permute-start | bytes 221192 | tf_op jit(solution)/shard_map/ppermute | solution.py:554
  59.8 20.1 %collective-permute-start.11 = (f32[80,8,256]{2,1,0:T(8,128)}, f32[80,8,256]{2,1,0:T(8,128)}, u32[]{:S(2)}, u32[]{:S(2)}) collective-permute-start(f32[80,8,256]{2,1,0:T(8,128)} %get-tuple-element.77.own_ref), channel_id=1, source_target_pairs={{0,16},{16,0},{1,17},{17,1},{2,18},{18,2},{3,19},{19,3},{4,20},{20... | collective-permute-start | bytes 1966088 | tf_op jit(solution)/shard_map/ppermute | solution.py:574
  65.8 17.7 %copy-start.11 = (f32[8,256]{1,0:T(8,128)S(1)}, f32[8,256]{1,0:T(8,128)}, u32[]{:S(2)}) copy-start(f32[8,256]{1,0:T(8,128)} %param.11) | copy-start | bytes 24580
  70.6 23.4 %collective-permute-start.13 = (f32[80,8,256]{2,1,0:T(8,128)}, f32[80,8,256]{2,1,0:T(8,128)}, u32[]{:S(2)}, u32[]{:S(2)}) collective-permute-start(f32[80,8,256]{2,1,0:T(8,128)} %get-tuple-element.91.own_ref), channel_id=1, source_target_pairs={{0,16},{16,0},{1,17},{17,1},{2,18},{18,2},{3,19},{19,3},{4,20},{20... | collective-permute-start | bytes 1966088 | tf_op jit(solution)/shard_map/ppermute | solution.py:574
  79.9 16.4 %copy-start.12 = (f32[8,256]{1,0:T(8,128)S(1)}, f32[8,256]{1,0:T(8,128)}, u32[]{:S(2)}) copy-start(f32[8,256]{1,0:T(8,128)} %param.10) | copy-start | bytes 24580
  83.1 25.0 %collective-permute-start.12 = (f32[81,8,256]{2,1,0:T(8,128)S(1)}, f32[81,8,256]{2,1,0:T(8,128)S(1)}, u32[]{:S(2)}, u32[]{:S(2)}) collective-permute-start(f32[81,8,256]{2,1,0:T(8,128)S(1)} %get-tuple-element.79.own_ref), channel_id=1, source_target_pairs={{0,16},{16,0},{1,17},{17,1},{2,18},{18,2},{3,19},{19,3},{4,20},{20... | collective-permute-start | bytes 1990664 | tf_op jit(solution)/shard_map/ppermute | solution.py:574
  93.9 16.4 %copy-start.3 = (f32[70,8,256]{2,1,0:T(8,128)S(1)}, f32[70,8,256]{2,1,0:T(8,128)}, u32[]{:S(2)}) copy-start(f32[70,8,256]{2,1,0:T(8,128)} %copy-done.2) | copy-start | bytes 1720324
  93.9 16.4 %copy-start.7 = (f32[70,8,256]{2,1,0:T(8,128)S(1)}, f32[70,8,256]{2,1,0:T(8,128)}, u32[]{:S(2)}) copy-start(f32[70,8,256]{2,1,0:T(8,128)} %copy-done.6) | copy-start | bytes 1720324
  94.0 16.4 %copy-start.9 = (f32[2,5,8,256]{3,2,1,0:T(8,128)S(1)}, f32[2,5,8,256]{3,2,1,0:T(8,128)}, u32[]{:S(2)}) copy-start(f32[2,5,8,256]{3,2,1,0:T(8,128)} %copy-done.8) | copy-start | bytes 245764
  95.9 26.2 %collective-permute-start.14 = (f32[80,8,256]{2,1,0:T(8,128)S(1)}, f32[80,8,256]{2,1,0:T(8,128)S(1)}, u32[]{:S(2)}, u32[]{:S(2)}) collective-permute-start(f32[80,8,256]{2,1,0:T(8,128)S(1)} %get-tuple-element.98.own_ref), channel_id=1, source_target_pairs={{0,16},{16,0},{1,17},{17,1},{2,18},{18,2},{3,19},{19,3},{4,20},{20... | collective-permute-start | bytes 1966088 | tf_op jit(solution)/shard_map/ppermute | solution.py:574
  109.9 26.3 %collective-permute-start.15 = (f32[80,8,256]{2,1,0:T(8,128)S(1)}, f32[80,8,256]{2,1,0:T(8,128)S(1)}, u32[]{:S(2)}, u32[]{:S(2)}) collective-permute-start(f32[80,8,256]{2,1,0:T(8,128)S(1)} %get-tuple-element.102.own_ref), channel_id=1, source_target_pairs={{0,16},{16,0},{1,17},{17,1},{2,18},{18,2},{3,19},{19,3},{4,20},{20... | collective-permute-start | bytes 1966088 | tf_op jit(solution)/shard_map/ppermute | solution.py:574
  112.1 12.2 %copy-start.1 = (f32[80,8,256]{2,1,0:T(8,128)S(1)}, f32[80,8,256]{2,1,0:T(8,128)}, u32[]{:S(2)}) copy-start(f32[80,8,256]{2,1,0:T(8,128)} %copy-done) | copy-start | bytes 1966084
  112.2 12.2 %copy-start.5 = (f32[80,8,256]{2,1,0:T(8,128)S(1)}, f32[80,8,256]{2,1,0:T(8,128)}, u32[]{:S(2)}) copy-start(f32[80,8,256]{2,1,0:T(8,128)} %copy-done.4) | copy-start | bytes 1966084
  123.9 26.3 %collective-permute-start.16 = (f32[80,8,256]{2,1,0:T(8,128)S(1)}, f32[80,8,256]{2,1,0:T(8,128)S(1)}, u32[]{:S(2)}, u32[]{:S(2)}) collective-permute-start(f32[80,8,256]{2,1,0:T(8,128)S(1)} %get-tuple-element.106.own_ref), channel_id=1, source_target_pairs={{0,16},{16,0},{1,17},{17,1},{2,18},{18,2},{3,19},{19,3},{4,20},{20... | collective-permute-start | bytes 1966088 | tf_op jit(solution)/shard_map/ppermute | solution.py:574
  137.4 18.4 %collective-permute-start.17 = (f32[32,8,256]{2,1,0:T(8,128)S(1)}, f32[32,8,256]{2,1,0:T(8,128)S(1)}, u32[]{:S(2)}, u32[]{:S(2)}) collective-permute-start(f32[32,8,256]{2,1,0:T(8,128)S(1)} %get-tuple-element.110.own_ref), channel_id=1, source_target_pairs={{0,16},{16,0},{1,17},{17,1},{2,18},{18,2},{3,19},{19,3},{4,20},{20... | collective-permute-start | bytes 786440 | tf_op jit(solution)/shard_map/ppermute | solution.py:574
  151.4 10.0 %collective-permute-start.18 = (f32[32,8,256]{2,1,0:T(8,128)S(1)}, f32[32,8,256]{2,1,0:T(8,128)S(1)}, u32[]{:S(2)}, u32[]{:S(2)}) collective-permute-start(f32[32,8,256]{2,1,0:T(8,128)S(1)} %get-tuple-element.114.own_ref), channel_id=1, source_target_pairs={{0,16},{16,0},{1,17},{17,1},{2,18},{18,2},{3,19},{19,3},{4,20},{20... | collective-permute-start | bytes 786440 | tf_op jit(solution)/shard_map/ppermute | solution.py:574
  156.9 7.4 %collective-permute-start.19 = (f32[16,8,256]{2,1,0:T(8,128)S(1)}, f32[16,8,256]{2,1,0:T(8,128)S(1)}, u32[]{:S(2)}, u32[]{:S(2)}) collective-permute-start(f32[16,8,256]{2,1,0:T(8,128)S(1)} %get-tuple-element.118.own_ref), channel_id=1, source_target_pairs={{0,16},{16,0},{1,17},{17,1},{2,18},{18,2},{3,19},{19,3},{4,20},{20... | collective-permute-start | bytes 393224 | tf_op jit(solution)/shard_map/ppermute | solution.py:574
  (1 other events, 0.8 us)

commit v2 on v0

--- a/solution.py
+++ b/solution.py
@@ -248,32 +248,37 @@
         copies = []
         for d in range(HALF_DIRS):
             for h in range(2):
+                place = h * HALF_DIRS + d
                 copy = pltpu.make_async_copy(
-                    spec_ref.at[d, pl.ds(first, count), :, pl.ds(128 * h, 128)], held.at[h * HALF_DIRS + d], sems.at[h * HALF_DIRS + d]
+                    spec_ref.at[pl.ds((d * NFREQ + first) * 8, count * 8), pl.ds(128 * h, 128)],
+                    held.at[pl.ds(place * count * 8, count * 8)],
+                    sems.at[place],
                 )
                 copy.start()
                 copies.append(copy)
-        rows = held.reshape((2 * HALF_DIRS + 1) * count * 8, 128)
         for d in range(HALF_DIRS):
             for h in range(2):
                 copies[2 * d + h].wait()
                 lanes_here = slice(128 * h, 128 * h + 128)
                 start = (h * HALF_DIRS + d) * count * 8
                 if d < LEAD_DIRS:
-                    column = rows[pl.ds(start + lead_row, count, stride=8), :]
+                    column = held[pl.ds(start + lead_row, count, stride=8), :]
                     lead_ref[d * count : (d + 1) * count, lanes_here] = column * sea_ref[lead_row : lead_row + 1, lanes_here]
                 elif d > LEAD_DIRS:
                     t = d - LEAD_DIRS - 1
-                    column = rows[pl.ds(start + trail_row, count, stride=8), :]
+                    column = held[pl.ds(start + trail_row, count, stride=8), :]
                     trail_ref[t * count : (t + 1) * count, lanes_here] = column * sea_ref[trail_row : trail_row + 1, lanes_here]
         lane = 0 if flipped else 127
         lanes = lax.broadcasted_iota(jnp.int32, (8, 128), 1)
         sea_line = jnp.broadcast_to(sea_ref[:, 128 * part + lane : 128 * part + lane + 1], (8, 128))
 
+        def slab(d, f):
+            return held[pl.ds(pl.multiple_of((part * HALF_DIRS + d) * count * 8 + f * 8, 8), 8), :]
+
         def one(f, kept):
             here = lanes == f
             return tuple(
-                jnp.where(here, jnp.broadcast_to(held[part * HALF_DIRS + d, f][:, lane : lane + 1], (8, 128)), kept[d])
+                jnp.where(here, jnp.broadcast_to(slab(d, f)[:, lane : lane + 1], (8, 128)), kept[d])
                 for d in range(HALF_DIRS)
             )
 
@@ -306,7 +311,7 @@
         in_specs=[vmem, hold, hold],
         out_specs=[vmem] * 3,
         scratch_shapes=[
-            pltpu.VMEM((2 * HALF_DIRS + 1, count, 8, 128), jnp.float32),
+            pltpu.VMEM(((2 * HALF_DIRS + 1) * count * 8, 128), jnp.float32),
             pltpu.SemaphoreType.DMA((2 * HALF_DIRS,)),
         ],
         compiler_params=pltpu.CompilerParams(vmem_limit_bytes=VMEM_BYTES),
@@ -558,13 +563,14 @@
     trail_pairs = joined(tiles_x, -1, True)
     lat_pairs = joined(tiles_y, 1, False)
 
+    rows = pltpu.with_memory_space_constraint(spectrum.reshape(HALF_DIRS * NFREQ * 8, 256), pltpu.HBM)
     spec = pltpu.with_memory_space_constraint(spec, pltpu.HBM)
     bounds = chunk_bounds()
     raw = raw_edges(spec)
 
     def halo(g, after):
         begin, end = HALO_GROUPS[g]
-        lead, trail, lat = pack(begin, end - begin, sea, spec, after)
+        lead, trail, lat = pack(begin, end - begin, sea, rows, after)
         sides = (
             lax.ppermute(lead, ("comp", "tx"), lead_pairs),
             lax.ppermute(trail, ("comp", "tx"), trail_pairs),

time: 165 us -> 165 us (level)
  no operation moved by 1% of the time
where the time goes in v2:
time: 165 us; the launch traced here: 164 us
  waiting for transfers between devices  70.5 us (43%)
  Pallas kernels  55.9 us (34%)
  starting transfers between devices  36.1 us (22%)
    ppermute x12, waiting for transfers between devices, send(): received.append(lax.ppermute(result[0], 'comp', swap))  53.3 us
    pallas_call x12, Pallas kernels, advect_chunk(): pl.pallas_call(functools.partial(advect_kernel, group, passes, carries, l...  26.3 us
    ppermute x12, starting transfers between devices, send(): received.append(lax.ppermute(result[0], 'comp', swap))  22.9 us
    pallas_call x12, Pallas kernels, source_chunk(): pl.pallas_call(functools.partial(source_kernel, first, count, inner, oute...  22 us
    ppermute x2, waiting for transfers between devices, halo(): lax.ppermute(trail, ('comp', 'tx'), trail_pairs)  11.6 us
    pallas_call x2, Pallas kernels, pack(): pl.pallas_call(functools.partial(pack_kernel, first, count), out_shape=[j...  6.51 us
    ppermute x2, starting transfers between devices, halo(): lax.ppermute(trail, ('comp', 'tx'), trail_pairs)  4.49 us
    ppermute x1, waiting for transfers between devices, paired_shards(): raw = lax.ppermute(raw, 'comp', swap)  3.83 us
  transfers between devices with their start and end apart: 19, of which 15 were waited for; matrix products, arithmetic and copies ran while one was open for 0% of the time, Pallas kernels for 33%

profile of v2, /device:TPU:0, one launch (start us, length us, event | category | flops | bytes accessed | tf_op | source)
XLA Modules:
  0.0 163.9 jit_solution(17445431714490530505)
XLA Ops:
  1.2 3.0 %collective-permute-start.3 = (f32[2,50,8,256]{3,2,1,0:T(8,128)S(1)}, f32[2,50,8,256]{3,2,1,0:T(8,128)S(1)}, u32[]{:S(2)}, u32[]{:S(2)}) collective-permute-start(f32[2,50,8,256]{3,2,1,0:T(8,128)S(1)} %shard_map.55.after_ref), channel_id=1, source_target_pairs={{0,16},{16,0},{1,17},{17,1},{2,18},{18,2},{3,19},{19,3},{4,20},{20... | collective-permute-start | bytes 2457608 | tf_op jit(solution)/shard_map/ppermute | solution.py:582
  4.2 2.5 %shard_map.56 = (f32[135,256]{1,0:T(8,128)S(1)}, f32[120,256]{1,0:T(8,128)S(1)}, f32[18,8,128]{2,1,0:T(8,128)S(1)}) custom-call(f32[8,256]{1,0:T(8,128)S(1)} %convert_element_type.7.sea_ref, f32[7200,256]{1,0:T(8,128)} %bitcast.10, f32[2,50,8,256]{3,2,1,0:T(8,128)S(1)} %shard_map.55.after_ref), custom_call_target="tpu_custom_call" | custom-call | flops 1024 | bytes 1024 | tf_op jit(solution)/shard_map/pallas_call | solution.py:304
  8.3 2.2 %collective-permute-start.1 = (f32[120,256]{1,0:T(8,128)S(1)}, f32[120,256]{1,0:T(8,128)S(1)}, u32[]{:S(2)}, u32[]{:S(2)}) collective-permute-start(f32[120,256]{1,0:T(8,128)S(1)} %get-tuple-element.64), channel_id=1, source_target_pairs={{0,12},{4,0},{8,4},{12,8},{16,20},{20,24},{24,28},{28,16},{1,13},{... | collective-permute-start | bytes 368648 | tf_op jit(solution)/shard_map/ppermute | solution.py:576
  12.7 3.1 %collective-permute-done.1.trail_ref = f32[120,256]{1,0:T(8,128)S(1)} collective-permute-done((f32[120,256]{1,0:T(8,128)S(1)}, f32[120,256]{1,0:T(8,128)S(1)}, u32[]{:S(2)}, u32[]{:S(2)}) %collective-permute-start.1) | collective-permute-done | bytes 122912 | tf_op jit(solution)/shard_map/ppermute | solution.py:576
  19.4 3.8 %collective-permute-done.3.rest_0_ = f32[2,50,8,256]{3,2,1,0:T(8,128)S(1)} collective-permute-done((f32[2,50,8,256]{3,2,1,0:T(8,128)S(1)}, f32[2,50,8,256]{3,2,1,0:T(8,128)S(1)}, u32[]{:S(2)}, u32[]{:S(2)}) %collective-permute-start.3) | collective-permute-done | bytes 819232 | tf_op jit(solution)/shard_map/ppermute | solution.py:582
  23.2 2.5 %shard_map.58 = (f32[90,8,256]{2,1,0:T(8,128)S(1)}, f32[2,5,8,256]{3,2,1,0:T(8,128)S(1)}, f32[8,256]{1,0:T(8,128)S(1)}) custom-call(f32[8,256]{1,0:T(8,128)S(1)} %convert_element_type.7.sea_ref, f32[2,8,256]{2,1,0:T(8,128)S(1)} %broadcast_multiply_fusion.slope_ref, f32[18,50,8,256]{3,2,1,0:T(8,128)} %bitcast.12, ...), custom_call_target="tpu_custom_call" | custom-call | flops 1024 | bytes 1024 | tf_op jit(solution)/shard_map/pallas_call | solution.py:449
  25.7 2.1 %collective-permute-start.8 = (f32[90,8,256]{2,1,0:T(8,128)S(1)}, f32[90,8,256]{2,1,0:T(8,128)S(1)}, u32[]{:S(2)}, u32[]{:S(2)}) collective-permute-start(f32[90,8,256]{2,1,0:T(8,128)S(1)} %get-tuple-element.73.rest_0_.own_ref), channel_id=1, source_target_pairs={{0,16},{16,0},{1,17},{17,1},{2,18},{18,2},{3,19},{19,3},{4,20},{20... | collective-permute-start | bytes 2211848 | tf_op jit(solution)/shard_map/ppermute | solution.py:597
  27.8 4.1 %shard_map.59 = (f32[315,256]{1,0:T(8,128)S(1)}, f32[280,256]{1,0:T(8,128)S(1)}, f32[18,8,128]{2,1,0:T(8,128)S(1)}) custom-call(f32[8,256]{1,0:T(8,128)S(1)} %convert_element_type.7.sea_ref, f32[7200,256]{1,0:T(8,128)} %bitcast.13, f32[8,256]{1,0:T(8,128)S(1)} %get-tuple-element.67.after_ref.steep_ref), custom_call_target="tpu_custom_call" | custom-call | flops 1024 | bytes 1024 | tf_op jit(solution)/shard_map/pallas_call | solution.py:304
  31.9 3.6 %collective-permute-done.7.rest_1_.other_ref = f32[70,8,256]{2,1,0:T(8,128)S(1)} collective-permute-done((f32[70,8,256]{2,1,0:T(8,128)S(1)}, f32[70,8,256]{2,1,0:T(8,128)S(1)}, u32[]{:S(2)}, u32[]{:S(2)}) %collective-permute-start.7) | collective-permute-done | bytes 573472 | tf_op jit(solution)/shard_map/ppermute | solution.py:597
  35.5 2.0 %shard_map.60 = (f32[80,8,256]{2,1,0:T(8,128)S(1)}, f32[2,5,8,256]{3,2,1,0:T(8,128)S(1)}, f32[8,256]{1,0:T(8,128)S(1)}) custom-call(f32[8,256]{1,0:T(8,128)S(1)} %convert_element_type.7.sea_ref, f32[2,8,256]{2,1,0:T(8,128)S(1)} %broadcast_multiply_fusion.slope_ref, f32[18,50,8,256]{3,2,1,0:T(8,128)} %bitcast.14, ...), custom_call_target="tpu_custom_call" | custom-call | flops 1024 | bytes 1024 | tf_op jit(solution)/shard_map/pallas_call | solution.py:449
  37.6 2.1 %collective-permute-start.9 = (f32[80,8,256]{2,1,0:T(8,128)S(1)}, f32[80,8,256]{2,1,0:T(8,128)S(1)}, u32[]{:S(2)}, u32[]{:S(2)}) collective-permute-start(f32[80,8,256]{2,1,0:T(8,128)S(1)} %get-tuple-element.75.own_ref), channel_id=1, source_target_pairs={{0,16},{16,0},{1,17},{17,1},{2,18},{18,2},{3,19},{19,3},{4,20},{20... | collective-permute-start | bytes 1966088 | tf_op jit(solution)/shard_map/ppermute | solution.py:597
  41.3 2.2 %collective-permute-start.5 = (f32[280,256]{1,0:T(8,128)S(1)}, f32[280,256]{1,0:T(8,128)S(1)}, u32[]{:S(2)}, u32[]{:S(2)}) collective-permute-start(f32[280,256]{1,0:T(8,128)S(1)} %get-tuple-element.69), channel_id=1, source_target_pairs={{0,12},{4,0},{8,4},{12,8},{16,20},{20,24},{24,28},{28,16},{1,13},{... | collective-permute-start | bytes 860168 | tf_op jit(solution)/shard_map/ppermute | solution.py:576
  45.7 8.6 %collective-permute-done.5.trail_ref = f32[280,256]{1,0:T(8,128)S(1)} collective-permute-done((f32[280,256]{1,0:T(8,128)S(1)}, f32[280,256]{1,0:T(8,128)S(1)}, u32[]{:S(2)}, u32[]{:S(2)}) %collective-permute-start.5) | collective-permute-done | bytes 286752 | tf_op jit(solution)/shard_map/ppermute | solution.py:576
  54.3 3.8 %shard_map.61 = (f32[80,8,256]{2,1,0:T(8,128)}, f32[2,5,8,256]{3,2,1,0:T(8,128)S(1)}, f32[8,256]{1,0:T(8,128)S(1)}) custom-call(f32[8,256]{1,0:T(8,128)S(1)} %convert_element_type.7.sea_ref, f32[2,8,256]{2,1,0:T(8,128)S(1)} %broadcast_multiply_fusion.slope_ref, f32[18,50,8,256]{3,2,1,0:T(8,128)} %bitcast.15, f32[315,256]{1,0:T(8,128)S(1)} %collective-permute-done.4.lead_ref, ...), custom_call_target="tpu_custom_call" | custom-call | flops 1024 | bytes 1024 | tf_op jit(solution)/shard_map/pallas_call | solution.py:449
  59.4 6.0 %collective-permute-done.9.rest_1_.other_ref = f32[80,8,256]{2,1,0:T(8,128)S(1)} collective-permute-done((f32[80,8,256]{2,1,0:T(8,128)S(1)}, f32[80,8,256]{2,1,0:T(8,128)S(1)}, u32[]{:S(2)}, u32[]{:S(2)}) %collective-permute-start.9) | collective-permute-done | bytes 655392 | tf_op jit(solution)/shard_map/ppermute | solution.py:597
  65.4 4.0 %shard_map.62 = (f32[80,8,256]{2,1,0:T(8,128)}, f32[2,5,8,256]{3,2,1,0:T(8,128)S(1)}, f32[8,256]{1,0:T(8,128)S(1)}) custom-call(f32[8,256]{1,0:T(8,128)S(1)} %convert_element_type.7.sea_ref, f32[2,8,256]{2,1,0:T(8,128)S(1)} %broadcast_multiply_fusion.slope_ref, f32[18,50,8,256]{3,2,1,0:T(8,128)} %bitcast.16, f32[315,256]{1,0:T(8,128)S(1)} %collective-permute-done.4.lead_ref, ...), custom_call_target="tpu_custom_call" | custom-call | flops 1024 | bytes 1024 | tf_op jit(solution)/shard_map/pallas_call | solution.py:449
  70.2 2.1 %collective-permute-start.12 = (f32[80,8,256]{2,1,0:T(8,128)}, f32[80,8,256]{2,1,0:T(8,128)}, u32[]{:S(2)}, u32[]{:S(2)}) collective-permute-start(f32[80,8,256]{2,1,0:T(8,128)} %get-tuple-element.91.own_ref), channel_id=1, source_target_pairs={{0,16},{16,0},{1,17},{17,1},{2,18},{18,2},{3,19},{19,3},{4,20},{20... | collective-permute-start | bytes 1966088 | tf_op jit(solution)/shard_map/ppermute | solution.py:597
  72.3 7.2 %collective-permute-done.10.rest_1_.other_ref = f32[80,8,256]{2,1,0:T(8,128)} collective-permute-done((f32[80,8,256]{2,1,0:T(8,128)}, f32[80,8,256]{2,1,0:T(8,128)}, u32[]{:S(2)}, u32[]{:S(2)}) %collective-permute-start.10) | collective-permute-done | bytes 655392 | tf_op jit(solution)/shard_map/ppermute | solution.py:597
  79.5 3.1 %shard_map.63 = (f32[81,8,256]{2,1,0:T(8,128)S(1)}, f32[2,5,8,256]{3,2,1,0:T(8,128)S(1)}, f32[8,256]{1,0:T(8,128)S(1)}) custom-call(f32[8,256]{1,0:T(8,128)S(1)} %convert_element_type.7.sea_ref, f32[2,8,256]{2,1,0:T(8,128)S(1)} %broadcast_multiply_fusion.slope_ref, f32[18,50,8,256]{3,2,1,0:T(8,128)} %bitcast.17, ...), custom_call_target="tpu_custom_call" | custom-call | flops 1024 | bytes 1024 | tf_op jit(solution)/shard_map/pallas_call | solution.py:449
  82.7 2.1 %collective-permute-start.11 = (f32[81,8,256]{2,1,0:T(8,128)S(1)}, f32[81,8,256]{2,1,0:T(8,128)S(1)}, u32[]{:S(2)}, u32[]{:S(2)}) collective-permute-start(f32[81,8,256]{2,1,0:T(8,128)S(1)} %get-tuple-element.79.own_ref), channel_id=1, source_target_pairs={{0,16},{16,0},{1,17},{17,1},{2,18},{18,2},{3,19},{19,3},{4,20},{20... | collective-permute-start | bytes 1990664 | tf_op jit(solution)/shard_map/ppermute | solution.py:597
  84.9 8.7 %collective-permute-done.12.other_ref.rest_1_ = f32[80,8,256]{2,1,0:T(8,128)} collective-permute-done((f32[80,8,256]{2,1,0:T(8,128)}, f32[80,8,256]{2,1,0:T(8,128)}, u32[]{:S(2)}, u32[]{:S(2)}) %collective-permute-start.12) | collective-permute-done | bytes 655392 | tf_op jit(solution)/shard_map/ppermute | solution.py:597
  95.5 2.1 %collective-permute-start.13 = (f32[80,8,256]{2,1,0:T(8,128)S(1)}, f32[80,8,256]{2,1,0:T(8,128)S(1)}, u32[]{:S(2)}, u32[]{:S(2)}) collective-permute-start(f32[80,8,256]{2,1,0:T(8,128)S(1)} %get-tuple-element.98.own_ref), channel_id=1, source_target_pairs={{0,16},{16,0},{1,17},{17,1},{2,18},{18,2},{3,19},{19,3},{4,20},{20... | collective-permute-start | bytes 1966088 | tf_op jit(solution)/shard_map/ppermute | solution.py:597
  97.6 10.1 %collective-permute-done.11.other_ref.rest_1_ = f32[81,8,256]{2,1,0:T(8,128)S(1)} collective-permute-done((f32[81,8,256]{2,1,0:T(8,128)S(1)}, f32[81,8,256]{2,1,0:T(8,128)S(1)}, u32[]{:S(2)}, u32[]{:S(2)}) %collective-permute-start.11) | collective-permute-done | bytes 663584 | tf_op jit(solution)/shard_map/ppermute | solution.py:597
  109.5 2.1 %collective-permute-start.14 = (f32[80,8,256]{2,1,0:T(8,128)S(1)}, f32[80,8,256]{2,1,0:T(8,128)S(1)}, u32[]{:S(2)}, u32[]{:S(2)}) collective-permute-start(f32[80,8,256]{2,1,0:T(8,128)S(1)} %get-tuple-element.102.own_ref), channel_id=1, source_target_pairs={{0,16},{16,0},{1,17},{17,1},{2,18},{18,2},{3,19},{19,3},{4,20},{20... | collective-permute-start | bytes 1966088 | tf_op jit(solution)/shard_map/ppermute | solution.py:597
  115.3 6.4 %collective-permute-done.13.other_ref.rest_1_ = f32[80,8,256]{2,1,0:T(8,128)S(1)} collective-permute-done((f32[80,8,256]{2,1,0:T(8,128)S(1)}, f32[80,8,256]{2,1,0:T(8,128)S(1)}, u32[]{:S(2)}, u32[]{:S(2)}) %collective-permute-start.13) | collective-permute-done | bytes 655392 | tf_op jit(solution)/shard_map/ppermute | solution.py:597
  123.6 2.1 %collective-permute-start.15 = (f32[80,8,256]{2,1,0:T(8,128)S(1)}, f32[80,8,256]{2,1,0:T(8,128)S(1)}, u32[]{:S(2)}, u32[]{:S(2)}) collective-permute-start(f32[80,8,256]{2,1,0:T(8,128)S(1)} %get-tuple-element.106.own_ref), channel_id=1, source_target_pairs={{0,16},{16,0},{1,17},{17,1},{2,18},{18,2},{3,19},{19,3},{4,20},{20... | collective-permute-start | bytes 1966088 | tf_op jit(solution)/shard_map/ppermute | solution.py:597
  127.5 3.1 %shard_map.67 = (f32[18,50,8,256]{3,2,1,0:T(8,128)}, f32[18,8,256]{2,1,0:T(8,128)S(1)}) custom-call(f32[2,8,256]{2,1,0:T(8,128)S(1)} %maximum_multiply_fusion.wind_ref, f32[8,256]{1,0:T(8,128)S(1)} %get-tuple-element.78.steep_a_ref.steep_ref, f32[8,256]{1,0:T(8,128)S(1)} %slice_bitcast_fusion.steep_b_ref, ...), custom_call_target="tpu_custom_call", output_to_operand_aliasing={{0}: (7, {})} | custom-call | flops 1024 | bytes 1024 | tf_op jit(solution)/shard_map/pallas_call | solution.py:525
  130.6 3.1 %shard_map.68 = (f32[18,50,8,256]{3,2,1,0:T(8,128)}, f32[18,8,256]{2,1,0:T(8,128)S(1)}) custom-call(f32[2,8,256]{2,1,0:T(8,128)S(1)} %maximum_multiply_fusion.wind_ref, f32[8,256]{1,0:T(8,128)S(1)} %get-tuple-element.78.steep_a_ref.steep_ref, f32[8,256]{1,0:T(8,128)S(1)} %slice_bitcast_fusion.steep_b_ref, ...), custom_call_target="tpu_custom_call", output_to_operand_aliasing={{0}: (7, {})} | custom-call | flops 1024 | bytes 1024 | tf_op jit(solution)/shard_map/pallas_call | solution.py:525
  133.7 2.1 %collective-permute-done.14.other_ref.rest_1_ = f32[80,8,256]{2,1,0:T(8,128)S(1)} collective-permute-done((f32[80,8,256]{2,1,0:T(8,128)S(1)}, f32[80,8,256]{2,1,0:T(8,128)S(1)}, u32[]{:S(2)}, u32[]{:S(2)}) %collective-permute-start.14) | collective-permute-done | bytes 655392 | tf_op jit(solution)/shard_map/ppermute | solution.py:597
  137.0 2.1 %collective-permute-start.16 = (f32[32,8,256]{2,1,0:T(8,128)S(1)}, f32[32,8,256]{2,1,0:T(8,128)S(1)}, u32[]{:S(2)}, u32[]{:S(2)}) collective-permute-start(f32[32,8,256]{2,1,0:T(8,128)S(1)} %get-tuple-element.110.own_ref), channel_id=1, source_target_pairs={{0,16},{16,0},{1,17},{17,1},{2,18},{18,2},{3,19},{19,3},{4,20},{20... | collective-permute-start | bytes 786440 | tf_op jit(solution)/shard_map/ppermute | solution.py:597
  142.8 7.0 %collective-permute-done.15.other_ref.rest_1_ = f32[80,8,256]{2,1,0:T(8,128)S(1)} collective-permute-done((f32[80,8,256]{2,1,0:T(8,128)S(1)}, f32[80,8,256]{2,1,0:T(8,128)S(1)}, u32[]{:S(2)}, u32[]{:S(2)}) %collective-permute-start.15) | collective-permute-done | bytes 655392 | tf_op jit(solution)/shard_map/ppermute | solution.py:597
  151.1 2.1 %collective-permute-start.17 = (f32[32,8,256]{2,1,0:T(8,128)S(1)}, f32[32,8,256]{2,1,0:T(8,128)S(1)}, u32[]{:S(2)}, u32[]{:S(2)}) collective-permute-start(f32[32,8,256]{2,1,0:T(8,128)S(1)} %get-tuple-element.114.own_ref), channel_id=1, source_target_pairs={{0,16},{16,0},{1,17},{17,1},{2,18},{18,2},{3,19},{19,3},{4,20},{20... | collective-permute-start | bytes 786440 | tf_op jit(solution)/shard_map/ppermute | solution.py:597
  (69 shorter events, 42.3 us)
Async XLA Ops:
  0.0 4.2 %copy-start.12 = (s32[8,256]{1,0:T(8,128)S(1)}, s32[8,256]{1,0:T(8,128)}, u32[]{:S(2)}) copy-start(s32[8,256]{1,0:T(8,128)} %param.8) | copy-start | bytes 24580
  0.0 11.8 %copy-start.10 = (f32[2,8,256]{2,1,0:T(8,128)S(1)}, f32[2,8,256]{2,1,0:T(8,128)}, u32[]{:S(2)}) copy-start(f32[2,8,256]{2,1,0:T(8,128)} %param.9) | copy-start | bytes 49156
  1.2 22.1 %collective-permute-start.3 = (f32[2,50,8,256]{3,2,1,0:T(8,128)S(1)}, f32[2,50,8,256]{3,2,1,0:T(8,128)S(1)}, u32[]{:S(2)}, u32[]{:S(2)}) collective-permute-start(f32[2,50,8,256]{3,2,1,0:T(8,128)S(1)} %shard_map.55.after_ref), channel_id=1, source_target_pairs={{0,16},{16,0},{1,17},{17,1},{2,18},{18,2},{3,19},{19,3},{4,20},{20... | collective-permute-start | bytes 2457608 | tf_op jit(solution)/shard_map/ppermute | solution.py:582
  6.7 9.1 %collective-permute-start = (f32[135,256]{1,0:T(8,128)S(1)}, f32[135,256]{1,0:T(8,128)S(1)}, u32[]{:S(2)}, u32[]{:S(2)}) collective-permute-start(f32[135,256]{1,0:T(8,128)S(1)} %get-tuple-element.63), channel_id=1, source_target_pairs={{0,4},{4,8},{8,12},{12,0},{16,28},{20,16},{24,20},{28,24},{1,5},{5... | collective-permute-start | bytes 414728 | tf_op jit(solution)/shard_map/ppermute | solution.py:575
  8.3 7.5 %collective-permute-start.1 = (f32[120,256]{1,0:T(8,128)S(1)}, f32[120,256]{1,0:T(8,128)S(1)}, u32[]{:S(2)}, u32[]{:S(2)}) collective-permute-start(f32[120,256]{1,0:T(8,128)S(1)} %get-tuple-element.64), channel_id=1, source_target_pairs={{0,12},{4,0},{8,4},{12,8},{16,20},{20,24},{24,28},{28,16},{1,13},{... | collective-permute-start | bytes 368648 | tf_op jit(solution)/shard_map/ppermute | solution.py:576
  10.5 2.2 %collective-permute-start.2 = (f32[18,8,128]{2,1,0:T(8,128)S(1)}, f32[18,8,128]{2,1,0:T(8,128)S(1)}, u32[]{:S(2)}, u32[]{:S(2)}) collective-permute-start(f32[18,8,128]{2,1,0:T(8,128)S(1)} %get-tuple-element.65), channel_id=1, source_target_pairs={{0,1},{1,2},{2,3},{17,16},{18,17},{19,18},{4,5},{5,6},{6,7},{21,20... | collective-permute-start | bytes 221192 | tf_op jit(solution)/shard_map/ppermute | solution.py:577
  17.6 10.3 %copy-start.8 = (f32[2,5,8,256]{3,2,1,0:T(8,128)}, f32[2,5,8,256]{3,2,1,0:T(8,128)S(1)}, u32[]{:S(2)}) copy-start(f32[2,5,8,256]{3,2,1,0:T(8,128)S(1)} %get-tuple-element.80.keep_ref) | copy-start | bytes 245764
  17.6 14.3 %copy-start.6 = (f32[70,8,256]{2,1,0:T(8,128)}, f32[70,8,256]{2,1,0:T(8,128)S(1)}, u32[]{:S(2)}) copy-start(f32[70,8,256]{2,1,0:T(8,128)S(1)} %get-tuple-element.71.own_ref) | copy-start | bytes 1720324
  17.6 17.9 %collective-permute-start.7 = (f32[70,8,256]{2,1,0:T(8,128)S(1)}, f32[70,8,256]{2,1,0:T(8,128)S(1)}, u32[]{:S(2)}, u32[]{:S(2)}) collective-permute-start(f32[70,8,256]{2,1,0:T(8,128)S(1)} %get-tuple-element.71.own_ref), channel_id=1, source_target_pairs={{0,16},{16,0},{1,17},{17,1},{2,18},{18,2},{3,19},{19,3},{4,20},{20... | collective-permute-start | bytes 1720328 | tf_op jit(solution)/shard_map/ppermute | solution.py:597
  25.7 28.6 %collective-permute-start.8 = (f32[90,8,256]{2,1,0:T(8,128)S(1)}, f32[90,8,256]{2,1,0:T(8,128)S(1)}, u32[]{:S(2)}, u32[]{:S(2)}) collective-permute-start(f32[90,8,256]{2,1,0:T(8,128)S(1)} %get-tuple-element.73.rest_0_.own_ref), channel_id=1, source_target_pairs={{0,16},{16,0},{1,17},{17,1},{2,18},{18,2},{3,19},{19,3},{4,20},{20... | collective-permute-start | bytes 2211848 | tf_op jit(solution)/shard_map/ppermute | solution.py:597
  35.5 18.8 %copy-start.2 = (f32[70,8,256]{2,1,0:T(8,128)}, f32[70,8,256]{2,1,0:T(8,128)S(1)}, u32[]{:S(2)}) copy-start(f32[70,8,256]{2,1,0:T(8,128)S(1)} %collective-permute-done.7.rest_1_.other_ref) | copy-start | bytes 1720324
  37.6 27.8 %copy-start.4 = (f32[80,8,256]{2,1,0:T(8,128)}, f32[80,8,256]{2,1,0:T(8,128)S(1)}, u32[]{:S(2)}) copy-start(f32[80,8,256]{2,1,0:T(8,128)S(1)} %get-tuple-element.75.own_ref) | copy-start | bytes 1966084
  37.6 27.8 %collective-permute-start.9 = (f32[80,8,256]{2,1,0:T(8,128)S(1)}, f32[80,8,256]{2,1,0:T(8,128)S(1)}, u32[]{:S(2)}, u32[]{:S(2)}) collective-permute-start(f32[80,8,256]{2,1,0:T(8,128)S(1)} %get-tuple-element.75.own_ref), channel_id=1, source_target_pairs={{0,16},{16,0},{1,17},{17,1},{2,18},{18,2},{3,19},{19,3},{4,20},{20... | collective-permute-start | bytes 1966088 | tf_op jit(solution)/shard_map/ppermute | solution.py:597
  39.7 14.6 %collective-permute-start.4 = (f32[315,256]{1,0:T(8,128)S(1)}, f32[315,256]{1,0:T(8,128)S(1)}, u32[]{:S(2)}, u32[]{:S(2)}) collective-permute-start(f32[315,256]{1,0:T(8,128)S(1)} %get-tuple-element.68.rest_2_), channel_id=1, source_target_pairs={{0,4},{4,8},{8,12},{12,0},{16,28},{20,16},{24,20},{28,24},{1,5},{5... | collective-permute-start | bytes 967688 | tf_op jit(solution)/shard_map/ppermute | solution.py:575
  41.3 13.0 %collective-permute-start.5 = (f32[280,256]{1,0:T(8,128)S(1)}, f32[280,256]{1,0:T(8,128)S(1)}, u32[]{:S(2)}, u32[]{:S(2)}) collective-permute-start(f32[280,256]{1,0:T(8,128)S(1)} %get-tuple-element.69), channel_id=1, source_target_pairs={{0,12},{4,0},{8,4},{12,8},{16,20},{20,24},{24,28},{28,16},{1,13},{... | collective-permute-start | bytes 860168 | tf_op jit(solution)/shard_map/ppermute | solution.py:576
  43.5 2.2 %collective-permute-start.6 = (f32[18,8,128]{2,1,0:T(8,128)S(1)}, f32[18,8,128]{2,1,0:T(8,128)S(1)}, u32[]{:S(2)}, u32[]{:S(2)}) collective-permute-start(f32[18,8,128]{2,1,0:T(8,128)S(1)} %get-tuple-element.70), channel_id=1, source_target_pairs={{0,1},{1,2},{2,3},{17,16},{18,17},{19,18},{4,5},{5,6},{6,7},{21,20... | collective-permute-start | bytes 221192 | tf_op jit(solution)/shard_map/ppermute | solution.py:577
  58.1 21.4 %collective-permute-start.10 = (f32[80,8,256]{2,1,0:T(8,128)}, f32[80,8,256]{2,1,0:T(8,128)}, u32[]{:S(2)}, u32[]{:S(2)}) collective-permute-start(f32[80,8,256]{2,1,0:T(8,128)} %get-tuple-element.77.own_ref), channel_id=1, source_target_pairs={{0,16},{16,0},{1,17},{17,1},{2,18},{18,2},{3,19},{19,3},{4,20},{20... | collective-permute-start | bytes 1966088 | tf_op jit(solution)/shard_map/ppermute | solution.py:597
  65.4 19.4 %copy-start.11 = (f32[8,256]{1,0:T(8,128)S(1)}, f32[8,256]{1,0:T(8,128)}, u32[]{:S(2)}) copy-start(f32[8,256]{1,0:T(8,128)} %param.11) | copy-start | bytes 24580
  70.2 23.3 %collective-permute-start.12 = (f32[80,8,256]{2,1,0:T(8,128)}, f32[80,8,256]{2,1,0:T(8,128)}, u32[]{:S(2)}, u32[]{:S(2)}) collective-permute-start(f32[80,8,256]{2,1,0:T(8,128)} %get-tuple-element.91.own_ref), channel_id=1, source_target_pairs={{0,16},{16,0},{1,17},{17,1},{2,18},{18,2},{3,19},{19,3},{4,20},{20... | collective-permute-start | bytes 1966088 | tf_op jit(solution)/shard_map/ppermute | solution.py:597
  79.5 18.1 %copy-start.13 = (f32[8,256]{1,0:T(8,128)S(1)}, f32[8,256]{1,0:T(8,128)}, u32[]{:S(2)}) copy-start(f32[8,256]{1,0:T(8,128)} %param.10) | copy-start | bytes 24580
  82.7 25.0 %collective-permute-start.11 = (f32[81,8,256]{2,1,0:T(8,128)S(1)}, f32[81,8,256]{2,1,0:T(8,128)S(1)}, u32[]{:S(2)}, u32[]{:S(2)}) collective-permute-start(f32[81,8,256]{2,1,0:T(8,128)S(1)} %get-tuple-element.79.own_ref), channel_id=1, source_target_pairs={{0,16},{16,0},{1,17},{17,1},{2,18},{18,2},{3,19},{19,3},{4,20},{20... | collective-permute-start | bytes 1990664 | tf_op jit(solution)/shard_map/ppermute | solution.py:597
  93.6 18.1 %copy-start.3 = (f32[70,8,256]{2,1,0:T(8,128)S(1)}, f32[70,8,256]{2,1,0:T(8,128)}, u32[]{:S(2)}) copy-start(f32[70,8,256]{2,1,0:T(8,128)} %copy-done.2) | copy-start | bytes 1720324
  93.6 18.1 %copy-start.7 = (f32[70,8,256]{2,1,0:T(8,128)S(1)}, f32[70,8,256]{2,1,0:T(8,128)}, u32[]{:S(2)}) copy-start(f32[70,8,256]{2,1,0:T(8,128)} %copy-done.6) | copy-start | bytes 1720324
  93.6 18.1 %copy-start.9 = (f32[2,5,8,256]{3,2,1,0:T(8,128)S(1)}, f32[2,5,8,256]{3,2,1,0:T(8,128)}, u32[]{:S(2)}) copy-start(f32[2,5,8,256]{3,2,1,0:T(8,128)} %copy-done.8) | copy-start | bytes 245764
  95.5 26.2 %collective-permute-start.13 = (f32[80,8,256]{2,1,0:T(8,128)S(1)}, f32[80,8,256]{2,1,0:T(8,128)S(1)}, u32[]{:S(2)}, u32[]{:S(2)}) collective-permute-start(f32[80,8,256]{2,1,0:T(8,128)S(1)} %get-tuple-element.98.own_ref), channel_id=1, source_target_pairs={{0,16},{16,0},{1,17},{17,1},{2,18},{18,2},{3,19},{19,3},{4,20},{20... | collective-permute-start | bytes 1966088 | tf_op jit(solution)/shard_map/ppermute | solution.py:597
  109.5 26.3 %collective-permute-start.14 = (f32[80,8,256]{2,1,0:T(8,128)S(1)}, f32[80,8,256]{2,1,0:T(8,128)S(1)}, u32[]{:S(2)}, u32[]{:S(2)}) collective-permute-start(f32[80,8,256]{2,1,0:T(8,128)S(1)} %get-tuple-element.102.own_ref), channel_id=1, source_target_pairs={{0,16},{16,0},{1,17},{17,1},{2,18},{18,2},{3,19},{19,3},{4,20},{20... | collective-permute-start | bytes 1966088 | tf_op jit(solution)/shard_map/ppermute | solution.py:597
  113.5 12.2 %copy-start.1 = (f32[80,8,256]{2,1,0:T(8,128)S(1)}, f32[80,8,256]{2,1,0:T(8,128)}, u32[]{:S(2)}) copy-start(f32[80,8,256]{2,1,0:T(8,128)} %copy-done) | copy-start | bytes 1966084
  113.5 12.2 %copy-start.5 = (f32[80,8,256]{2,1,0:T(8,128)S(1)}, f32[80,8,256]{2,1,0:T(8,128)}, u32[]{:S(2)}) copy-start(f32[80,8,256]{2,1,0:T(8,128)} %copy-done.4) | copy-start | bytes 1966084
  123.6 26.3 %collective-permute-start.15 = (f32[80,8,256]{2,1,0:T(8,128)S(1)}, f32[80,8,256]{2,1,0:T(8,128)S(1)}, u32[]{:S(2)}, u32[]{:S(2)}) collective-permute-start(f32[80,8,256]{2,1,0:T(8,128)S(1)} %get-tuple-element.106.own_ref), channel_id=1, source_target_pairs={{0,16},{16,0},{1,17},{17,1},{2,18},{18,2},{3,19},{19,3},{4,20},{20... | collective-permute-start | bytes 1966088 | tf_op jit(solution)/shard_map/ppermute | solution.py:597
  137.0 19.8 %collective-permute-start.16 = (f32[32,8,256]{2,1,0:T(8,128)S(1)}, f32[32,8,256]{2,1,0:T(8,128)S(1)}, u32[]{:S(2)}, u32[]{:S(2)}) collective-permute-start(f32[32,8,256]{2,1,0:T(8,128)S(1)} %get-tuple-element.110.own_ref), channel_id=1, source_target_pairs={{0,16},{16,0},{1,17},{17,1},{2,18},{18,2},{3,19},{19,3},{4,20},{20... | collective-permute-start | bytes 786440 | tf_op jit(solution)/shard_map/ppermute | solution.py:597
  151.1 10.0 %collective-permute-start.17 = (f32[32,8,256]{2,1,0:T(8,128)S(1)}, f32[32,8,256]{2,1,0:T(8,128)S(1)}, u32[]{:S(2)}, u32[]{:S(2)}) collective-permute-start(f32[32,8,256]{2,1,0:T(8,128)S(1)} %get-tuple-element.114.own_ref), channel_id=1, source_target_pairs={{0,16},{16,0},{1,17},{17,1},{2,18},{18,2},{3,19},{19,3},{4,20},{20... | collective-permute-start | bytes 786440 | tf_op jit(solution)/shard_map/ppermute | solution.py:597
  157.9 5.1 %collective-permute-start.18 = (f32[16,8,256]{2,1,0:T(8,128)S(1)}, f32[16,8,256]{2,1,0:T(8,128)S(1)}, u32[]{:S(2)}, u32[]{:S(2)}) collective-permute-start(f32[16,8,256]{2,1,0:T(8,128)S(1)} %get-tuple-element.118.own_ref), channel_id=1, source_target_pairs={{0,16},{16,0},{1,17},{17,1},{2,18},{18,2},{3,19},{19,3},{4,20},{20... | collective-permute-start | bytes 393224 | tf_op jit(solution)/shard_map/ppermute | solution.py:597
  (1 other events, 0.8 us)
